TPU v7x, 32 devices: a whole 2x2x4 slice. The times are simulated.
32 devices in a mesh: dp: 4 (over y, core), seq: 8 (over z, x).
Axes of the slice: x: 2, y: 2, z: 4, core: 2. Of those that a mesh axis runs over, the one named last changes fastest.
Arguments:
- tokens: bfloat16 [32, 2048, 512], P('dp', 'seq'), may hold values from -6 to 6
- cotangent: bfloat16 [32, 2048, 512], P('dp', 'seq'), may hold values from -6 to 6
- lengths: int32 [32], P('dp'), may hold values from 512 to 2048, as said below
- w_qkv: float32 [512, 1536], P(('dp', 'seq')), may hold values from -0.25 to 0.25
- w_out: float32 [512, 512], P(('dp', 'seq')), may hold values from -0.375 to 0.375
- w_up: float32 [512, 2048], P(('dp', 'seq')), may hold values from -0.25 to 0.25
- w_down: float32 [2048, 512], P(('dp', 'seq')), may hold values from -0.125 to 0.125
- norm_params: float32 [4, 512], P(None, ('dp', 'seq')), may hold values from -1.5 to 2.5
- first_qkv: float32 [512, 1536], P(('dp', 'seq')), may hold values from -0.00036621094 to 0.00036621094
- first_out: float32 [512, 512], P(('dp', 'seq')), may hold values from -0.00036621094 to 0.00036621094
- first_up: float32 [512, 2048], P(('dp', 'seq')), may hold values from -0.00036621094 to 0.00036621094
- first_down: float32 [2048, 512], P(('dp', 'seq')), may hold values from -0.00036621094 to 0.00036621094
- first_norm: float32 [4, 512], P(None, ('dp', 'seq')), may hold values from -0.0009765625 to 0.0009765625
- second_qkv: float32 [512, 1536], P(('dp', 'seq')), may hold values from 3.1789144e-10 to 1.2715657e-09
- second_out: float32 [512, 512], P(('dp', 'seq')), may hold values from 3.1789144e-10 to 1.2715657e-09
- second_up: float32 [512, 2048], P(('dp', 'seq')), may hold values from 3.1789144e-10 to 1.2715657e-09
- second_down: float32 [2048, 512], P(('dp', 'seq')), may hold values from 3.1789144e-10 to 1.2715657e-09
- second_norm: float32 [4, 512], P(None, ('dp', 'seq')), may hold values from 2.861023e-09 to 1.1444092e-08
Outputs:
- activations: bfloat16 [32, 2048, 512], P('dp', 'seq')
- input_grad: float32 [32, 2048, 512], P('dp', 'seq')
- grad_norm: float32 [], replicated
- new_qkv: float32 [512, 1536], P(('dp', 'seq'))
- new_first_qkv: float32 [512, 1536], P(('dp', 'seq'))
- new_second_qkv: float32 [512, 1536], P(('dp', 'seq'))
- new_out: float32 [512, 512], P(('dp', 'seq'))
- new_first_out: float32 [512, 512], P(('dp', 'seq'))
- new_second_out: float32 [512, 512], P(('dp', 'seq'))
- new_up: float32 [512, 2048], P(('dp', 'seq'))
- new_first_up: float32 [512, 2048], P(('dp', 'seq'))
- new_second_up: float32 [512, 2048], P(('dp', 'seq'))
- new_down: float32 [2048, 512], P(('dp', 'seq'))
- new_first_down: float32 [2048, 512], P(('dp', 'seq'))
- new_second_down: float32 [2048, 512], P(('dp', 'seq'))
- new_norm: float32 [4, 512], P(None, ('dp', 'seq'))
- new_first_norm: float32 [4, 512], P(None, ('dp', 'seq'))
- new_second_norm: float32 [4, 512], P(None, ('dp', 'seq'))
Inputs may be any that keep to these rules, and one draw needn't show every extreme that they name: `lengths`: in each group of 8 consecutive items one item has length 2048.
All inputs are finite; a program needn't handle non-finite values.
Results may differ from a plain program's by a relative error of at most 0.0086.
Values may be sent and summed in bfloat16 or wider, within the bound.
A program may use at most 192 MiB of HBM per device.

v0:
```python
import jax
import jax.numpy as jnp
from jax import lax
from jax.sharding import PartitionSpec as P

HEADS = 8
HEAD_DIM = 64
SPAN = 128
STEP = 10


eps_norm = 1e-05
neg_fill = -1e30
beta_one = 0.9
beta_two = 0.999
adam_eps = 1e-08
decay_coef = 0.1
rate_matrix = 0.05
rate_norm = 0.5
clip_bound = 1.0


def normalize(values_in, gain_row, shift_row):
    center = values_in - jnp.mean(values_in, axis=-1, keepdims=True)
    spread = jnp.mean(center * center, axis=-1, keepdims=True)
    return center * lax.rsqrt(spread + eps_norm) * gain_row + shift_row


def adamw_update(weight, grad_in, first_old, second_old, factor, step_rate, weight_decay):
    clipped = grad_in * factor
    first_new = beta_one * first_old + (1.0 - beta_one) * clipped
    second_new = beta_two * second_old + (1.0 - beta_two) * clipped * clipped
    first_hat = first_new / (1.0 - beta_one**STEP)
    second_hat = second_new / (1.0 - beta_two**STEP)
    weight_new = weight - step_rate * (
        first_hat / (jnp.sqrt(second_hat) + adam_eps) + weight_decay * weight
    )
    return (weight_new, first_new, second_new)


def per_device(
    tokens,
    cotangent,
    lengths,
    w_qkv,
    w_out,
    w_up,
    w_down,
    norm_params,
    first_qkv,
    first_out,
    first_up,
    first_down,
    first_norm,
    second_qkv,
    second_out,
    second_up,
    second_down,
    second_norm,
):
    item_count, local_len, model_width = tokens.shape
    row_count = item_count * local_len
    spans_here = local_len // SPAN
    spans_all = spans_here * lax.axis_size("seq")
    seq_rank = lax.axis_index("seq")
    score_scale = HEAD_DIM ** (-0.5)
    full_qkv, full_out, full_up, full_down, full_norm = (
        lax.all_gather(w_qkv.astype(jnp.bfloat16), ("dp", "seq"), axis=0, tiled=True),
        lax.all_gather(w_out.astype(jnp.bfloat16), ("dp", "seq"), axis=0, tiled=True),
        lax.all_gather(w_up.astype(jnp.bfloat16), ("dp", "seq"), axis=0, tiled=True),
        lax.all_gather(w_down.astype(jnp.bfloat16), ("dp", "seq"), axis=0, tiled=True),
        lax.all_gather(norm_params.astype(jnp.bfloat16), ("dp", "seq"), axis=1, tiled=True),
    )
    norm_rows = full_norm.astype(jnp.float32)
    tokens_f = tokens.reshape(row_count, model_width).astype(jnp.float32)
    normed, back_one = jax.vjp(normalize, tokens_f, norm_rows[0], norm_rows[1])
    normed_b = normed.astype(jnp.bfloat16)
    qkv_b = jnp.dot(normed_b, full_qkv, preferred_element_type=jnp.float32).astype(jnp.bfloat16)
    qkv_view = qkv_b.reshape(item_count, spans_here, SPAN, 3, HEADS, HEAD_DIM)
    query_part = qkv_view[:, :, :, 0]
    key_part = qkv_view[:, :, :, 1]
    value_part = qkv_view[:, :, :, 2]
    local_pos = seq_rank * local_len + jnp.arange(local_len, dtype=jnp.int32)
    live_mask = (local_pos[None, :] < lengths[:, None]).reshape(item_count, spans_here, SPAN)
    live_f = live_mask.astype(jnp.float32)
    counts_here = jnp.maximum(jnp.sum(live_f, axis=2), 1.0)
    pooled = jnp.einsum(
        "ist,istchd->ischd",
        live_mask.astype(jnp.bfloat16),
        qkv_view[:, :, :, 1:],
        preferred_element_type=jnp.float32,
    )
    pooled = (pooled / counts_here[:, :, None, None, None]).astype(jnp.bfloat16)
    pooled_all = lax.all_gather(pooled, "seq", axis=1, tiled=True)
    pooled_keys = pooled_all[:, :, 0]
    pooled_values = pooled_all[:, :, 1]
    all_pos = jnp.arange(spans_all * SPAN, dtype=jnp.int32).reshape(spans_all, SPAN)
    counts_all = jnp.sum((all_pos[None] < lengths[:, None, None]).astype(jnp.float32), axis=2)
    span_ids = seq_rank * spans_here + jnp.arange(spans_here, dtype=jnp.int32)
    far_valid = (counts_all[:, None, :] > 0.0) & (
        span_ids[None, :, None] != jnp.arange(spans_all, dtype=jnp.int32)[None, None, :]
    )
    near_mask = live_mask[:, :, None, None, :]
    far_mask = far_valid[:, :, None, None, :]

    def scores_of():
        near_raw = (
            jnp.einsum(
                "isqhd,iskhd->ishqk", query_part, key_part, preferred_element_type=jnp.float32
            )
            * score_scale
        )
        far_raw = (
            jnp.einsum(
                "isqhd,irhd->ishqr", query_part, pooled_keys, preferred_element_type=jnp.float32
            )
            * score_scale
        )
        return (jnp.where(near_mask, near_raw, neg_fill), jnp.where(far_mask, far_raw, neg_fill))

    near_s, far_s = scores_of()
    score_top = jnp.maximum(
        jnp.max(near_s, axis=-1, keepdims=True), jnp.max(far_s, axis=-1, keepdims=True)
    )
    exp_total = jnp.sum(jnp.exp(near_s - score_top), axis=-1, keepdims=True) + jnp.sum(
        jnp.exp(far_s - score_top), axis=-1, keepdims=True
    )
    log_total = score_top + jnp.log(exp_total)
    near_pb = jnp.exp(near_s - log_total).astype(jnp.bfloat16)
    far_pb = jnp.exp(far_s - log_total).astype(jnp.bfloat16)
    mixed_rows = jnp.einsum(
        "ishqk,iskhd->isqhd", near_pb, value_part, preferred_element_type=jnp.float32
    )
    mixed_rows = mixed_rows + jnp.einsum(
        "ishqr,irhd->isqhd", far_pb, pooled_values, preferred_element_type=jnp.float32
    )
    mixed_b = mixed_rows.reshape(row_count, model_width).astype(jnp.bfloat16)
    residual = tokens_f + jnp.dot(mixed_b, full_out, preferred_element_type=jnp.float32)
    normed_two, back_two = jax.vjp(normalize, residual, norm_rows[2], norm_rows[3])
    normed_two_b = normed_two.astype(jnp.bfloat16)
    up_pre = jnp.dot(normed_two_b, full_up, preferred_element_type=jnp.float32)
    gated, gelu_back = jax.vjp(jax.nn.gelu, up_pre)
    gated_b = gated.astype(jnp.bfloat16)
    layer_out = residual + jnp.dot(gated_b, full_down, preferred_element_type=jnp.float32)
    activations = layer_out.astype(jnp.bfloat16).reshape(item_count, local_len, model_width)
    grad_out_b = cotangent.reshape(row_count, model_width)
    grad_down = jnp.dot(gated_b.T, grad_out_b, preferred_element_type=jnp.float32)
    grad_gated = jnp.dot(grad_out_b, full_down.T, preferred_element_type=jnp.float32)
    grad_up_pre = gelu_back(grad_gated)[0].astype(jnp.bfloat16)
    grad_up = jnp.dot(normed_two_b.T, grad_up_pre, preferred_element_type=jnp.float32)
    grad_normed_two = jnp.dot(grad_up_pre, full_up.T, preferred_element_type=jnp.float32)
    grad_resid_ln, grad_gain_two, grad_shift_two = back_two(grad_normed_two)
    grad_resid = grad_out_b.astype(jnp.float32) + grad_resid_ln
    grad_attn_b = grad_resid.astype(jnp.bfloat16)
    grad_out_proj = jnp.dot(mixed_b.T, grad_attn_b, preferred_element_type=jnp.float32)
    grad_mixed = jnp.dot(grad_attn_b, full_out.T, preferred_element_type=jnp.float32).astype(
        jnp.bfloat16
    )
    grad_mixed = grad_mixed.reshape(item_count, spans_here, SPAN, HEADS, HEAD_DIM)
    near_s, far_s = scores_of()
    near_pf = jnp.exp(near_s - log_total)
    far_pf = jnp.exp(far_s - log_total)
    near_pb = near_pf.astype(jnp.bfloat16)
    far_pb = far_pf.astype(jnp.bfloat16)
    grad_near = jnp.einsum(
        "isqhd,iskhd->ishqk", grad_mixed, value_part, preferred_element_type=jnp.float32
    )
    grad_far = jnp.einsum(
        "isqhd,irhd->ishqr", grad_mixed, pooled_values, preferred_element_type=jnp.float32
    )
    row_delta = jnp.sum(near_pf * grad_near, axis=-1, keepdims=True) + jnp.sum(
        far_pf * grad_far, axis=-1, keepdims=True
    )
    dscore_near = (near_pf * (grad_near - row_delta)).astype(jnp.bfloat16)
    dscore_far = (far_pf * (grad_far - row_delta)).astype(jnp.bfloat16)
    grad_query = jnp.einsum(
        "ishqk,iskhd->isqhd", dscore_near, key_part, preferred_element_type=jnp.float32
    )
    grad_query = (
        grad_query
        + jnp.einsum(
            "ishqr,irhd->isqhd", dscore_far, pooled_keys, preferred_element_type=jnp.float32
        )
    ) * score_scale
    grad_keys = (
        jnp.einsum(
            "ishqk,isqhd->iskhd", dscore_near, query_part, preferred_element_type=jnp.float32
        )
        * score_scale
    )
    grad_values = jnp.einsum(
        "ishqk,isqhd->iskhd", near_pb, grad_mixed, preferred_element_type=jnp.float32
    )
    grad_pool_keys = (
        jnp.einsum("ishqr,isqhd->irhd", dscore_far, query_part, preferred_element_type=jnp.float32)
        * score_scale
    )
    grad_pool_values = jnp.einsum(
        "ishqr,isqhd->irhd", far_pb, grad_mixed, preferred_element_type=jnp.float32
    )
    pool_grads = jnp.stack([grad_pool_keys, grad_pool_values], axis=2)
    pool_mine = lax.psum_scatter(
        pool_grads.astype(jnp.bfloat16), "seq", scatter_dimension=1, tiled=True
    ).astype(jnp.float32)
    spread_back = pool_mine / counts_here[:, :, None, None, None]
    grad_kv = (
        jnp.stack([grad_keys, grad_values], axis=3)
        + live_f[:, :, :, None, None, None] * spread_back[:, :, None]
    )
    grad_qkv_rows = jnp.concatenate([grad_query[:, :, :, None], grad_kv], axis=3)
    grad_qkv_b = grad_qkv_rows.reshape(row_count, 3 * model_width).astype(jnp.bfloat16)
    grad_qkv = jnp.dot(normed_b.T, grad_qkv_b, preferred_element_type=jnp.float32)
    grad_normed = jnp.dot(grad_qkv_b, full_qkv.T, preferred_element_type=jnp.float32)
    grad_in_ln, grad_gain_one, grad_shift_one = back_one(grad_normed)
    input_grad = (grad_resid + grad_in_ln).reshape(item_count, local_len, model_width)
    grad_norm_rows = jnp.stack([grad_gain_one, grad_shift_one, grad_gain_two, grad_shift_two])
    red_qkv, red_out, red_up, red_down, red_norm = (
        lax.psum_scatter(grad_qkv, ("dp", "seq"), scatter_dimension=0, tiled=True),
        lax.psum_scatter(grad_out_proj, ("dp", "seq"), scatter_dimension=0, tiled=True),
        lax.psum_scatter(grad_up, ("dp", "seq"), scatter_dimension=0, tiled=True),
        lax.psum_scatter(grad_down, ("dp", "seq"), scatter_dimension=0, tiled=True),
        lax.psum_scatter(grad_norm_rows, ("dp", "seq"), scatter_dimension=1, tiled=True),
    )
    squares = jnp.sum(red_qkv * red_qkv) + jnp.sum(red_out * red_out) + jnp.sum(red_up * red_up)
    squares = squares + jnp.sum(red_down * red_down) + jnp.sum(red_norm * red_norm)
    total_sq = lax.psum(squares, ("dp", "seq"))
    grad_norm = jnp.sqrt(total_sq)
    factor = clip_bound / jnp.maximum(grad_norm, clip_bound)
    new_qkv, new_first_qkv, new_second_qkv = adamw_update(
        w_qkv, red_qkv, first_qkv, second_qkv, factor, rate_matrix, decay_coef
    )
    new_out, new_first_out, new_second_out = adamw_update(
        w_out, red_out, first_out, second_out, factor, rate_matrix, decay_coef
    )
    new_up, new_first_up, new_second_up = adamw_update(
        w_up, red_up, first_up, second_up, factor, rate_matrix, decay_coef
    )
    new_down, new_first_down, new_second_down = adamw_update(
        w_down, red_down, first_down, second_down, factor, rate_matrix, decay_coef
    )
    new_norm, new_first_norm, new_second_norm = adamw_update(
        norm_params, red_norm, first_norm, second_norm, factor, rate_norm, 0.0
    )
    return (
        activations,
        input_grad,
        grad_norm,
        new_qkv,
        new_first_qkv,
        new_second_qkv,
        new_out,
        new_first_out,
        new_second_out,
        new_up,
        new_first_up,
        new_second_up,
        new_down,
        new_first_down,
        new_second_down,
        new_norm,
        new_first_norm,
        new_second_norm,
    )


def solution(mesh):
    placed = (
        P("dp", "seq", None),
        P("dp", "seq", None),
        P("dp"),
        P(("dp", "seq"), None),
        P(("dp", "seq"), None),
        P(("dp", "seq"), None),
        P(("dp", "seq"), None),
        P(None, ("dp", "seq")),
        P(("dp", "seq"), None),
        P(("dp", "seq"), None),
        P(("dp", "seq"), None),
        P(("dp", "seq"), None),
        P(None, ("dp", "seq")),
        P(("dp", "seq"), None),
        P(("dp", "seq"), None),
        P(("dp", "seq"), None),
        P(("dp", "seq"), None),
        P(None, ("dp", "seq")),
    )
    return jax.shard_map(
        per_device,
        mesh=mesh,
        in_specs=placed,
        out_specs=(
            P("dp", "seq", None),
            P("dp", "seq", None),
            P(),
            P(("dp", "seq"), None),
            P(("dp", "seq"), None),
            P(("dp", "seq"), None),
            P(("dp", "seq"), None),
            P(("dp", "seq"), None),
            P(("dp", "seq"), None),
            P(("dp", "seq"), None),
            P(("dp", "seq"), None),
            P(("dp", "seq"), None),
            P(("dp", "seq"), None),
            P(("dp", "seq"), None),
            P(("dp", "seq"), None),
            P(None, ("dp", "seq")),
            P(None, ("dp", "seq")),
            P(None, ("dp", "seq")),
        ),
        check_vma=False,
    )
```

profile of v0, /device:TPU:0, one launch (start us, length us, event | category | flops | bytes accessed | tf_op | source)
XLA Modules:
  0.0 1166.9 jit_solution(5028430925094048010)
XLA Ops:
  15.1 69.7 %all-gather = bf16[32,16,4]{1,2,0:T(4,128)(2,1)S(1)} all-gather(bf16[1,16,4]{1,2,0:T(4,128)(2,1)S(1)} %convert_bitcast_fusion), channel_id=1, replica_groups=mesh['dp'=4,'seq'=8] {'dp','seq'}, dimensions={0}, use_global_device_ids=true | all-gather | bytes 4224 | tf_op jit(solution)/shard_map/all_gather | solution.py:72
  90.2 72.0 %all_gather.21 = bf16[512,512]{1,0:T(8,128)(2,1)} all-gather(bf16[16,512]{1,0:T(8,128)(2,1)S(1)} %convert_element_type.127), channel_id=1, replica_groups=mesh['dp'=4,'seq'=8] {'dp','seq'}, dimensions={0}, use_global_device_ids=true | all-gather | bytes 540672 | tf_op jit(solution)/shard_map/all_gather | solution.py:69
  164.1 8.1 convolution_convert_fusion
  172.3 8.7 copy.170
  181.0 11.0 reshape.279
  191.9 7.5 fusion.120
  199.5 2.2 slice-done.2
  201.6 3.4 fusion.27
  205.1 31.5 %all_gather.20 = bf16[8,16,2,8,64]{4,3,2,0,1:T(8,128)(2,1)S(1)} all-gather(bf16[8,2,2,8,64]{4,3,2,0,1:T(8,128)(2,1)S(1)} %fusion.92), channel_id=1, replica_groups=mesh['dp'=4,'seq'=8] {'seq'}, dimensions={1}, use_global_device_ids=true | all-gather | bytes 294912 | tf_op jit(solution)/shard_map/all_gather | solution.py:94
  236.8 3.2 fusion.7
  240.9 2.6 exponential_reduce_fusion
  244.0 3.1 fusion.35
  248.0 3.5 copy.184
  251.5 4.5 convert_element_type.126
  256.0 3.1 fusion.124
  259.1 2.0 copy-done.2
  262.5 14.5 %multiply_convert_fusion = (bf16[2048,2048]{1,0:T(8,128)(2,1)}, f32[2048,2048]{1,0:T(8,128)}) fusion(bf16[512,2048]{1,0:T(8,128)(2,1)} %all-gather.7.cloned.1.call-done, f32[2048,512]{1,0:T(8,128)} %copy-done.2, f32[512]{0:T(512)} %bitcast.241, f32[512]{0:T(512)} %bitcast.237, f32[2048]{0:T(1024)} %fusion.102, f32[2048]{0:T(1024)} %copy-done.44), kind=kOutput, calls=%fused_computation.9 | convolution fusion | flops 4337958912 | bytes 31477760 | tf_op jit(solution)/shard_map/dot_general | solution.py:141
  277.1 20.2 %fusion.6 = bf16[2048,2048]{1,0:T(8,128)(2,1)} fusion(f32[2048,2048]{1,0:T(8,128)} %get-tuple-element.64, bf16[2048,512]{1,0:T(8,128)(2,1)} %bitcast.215, bf16[2048,512]{1,0:T(8,128)(2,1)} %all-gather.9.cloned.1.call-done), kind=kOutput, calls=%fused_computation.8 | convolution fusion | flops 4378853376 | bytes 29360128 | tf_op jit(solution)/shard_map/dot_general | solution.py:148
  297.4 8.8 multiply_reduce_fusion.1
  311.2 2.7 convolution_convert_fusion.1
  313.9 4.0 copy.185
  317.9 4.5 reshape.282
  322.3 3.5 multiply_reduce_fusion.4
  325.9 9.1 multiply_reduce_fusion
  335.7 5.1 convolution_bitcast_fusion
  340.9 2.9 multiply_convert_fusion.1
  343.8 3.4 fusion.37
  350.0 4.6 fusion.10
  354.6 5.0 multiply_bitcast_fusion
  359.6 50.4 %reduce-scatter.9.cloned.1.call-done = bf16[8,2,2,8,64]{4,3,2,0,1:T(8,128)(2,1)} async-done(((bf16[8,16,2,8,64]{4,3,2,0,1:T(8,128)(2,1)}), bf16[8,2,2,8,64]{4,3,2,0,1:T(8,128)(2,1)}) %reduce-scatter.9.cloned.1.call-update) | async-done | bytes 32784 | tf_op jit(solution)/shard_map/reduce_scatter | solution.py:202
  410.0 5.1 maximum_add_fusion
  415.1 2.1 maximum_convert_fusion
  417.3 6.0 copy.199
  423.2 11.1 convert_element_type.141
  434.4 6.8 fusion.26
  443.3 2.2 fusion.21
  446.5 4.5 fusion.126
  452.1 7.9 fusion.125
  460.2 11.4 fusion.112
  471.7 10.5 fusion.127
  482.3 11.1 add_convert_fusion
  493.4 85.7 %reduce-scatter.19.cloned.1.call-done = f32[16,4]{1,0:T(8,128)} async-done(((f32[512,4]{1,0:T(8,128)}), f32[16,4]{1,0:T(8,128)}) %reduce-scatter.19.cloned.1.call-update) | async-done | bytes 272
  580.5 132.0 %reduce-scatter.13.cloned.1.call-done = f32[16,512]{1,0:T(8,128)} async-done(((f32[512,512]{1,0:T(8,128)}), f32[16,512]{1,0:T(8,128)}) %reduce-scatter.13.cloned.1.call-update) | async-done | bytes 32784 | tf_op jit(solution)/shard_map/reduce_scatter | solution.py:219
  713.9 102.8 %reduce-scatter.11.cloned.1.call-done = f32[16,1536]{1,0:T(8,128)} async-done(((f32[512,1536]{1,0:T(8,128)}), f32[16,1536]{1,0:T(8,128)}) %reduce-scatter.11.cloned.1.call-update) | async-done | bytes 98320 | tf_op jit(solution)/shard_map/reduce_scatter | solution.py:218
  819.5 142.5 %reduce-scatter.15.cloned.1.call-done = f32[16,2048]{1,0:T(8,128)} async-done(((f32[512,2048]{1,0:T(8,128)}), f32[16,2048]{1,0:T(8,128)}) %reduce-scatter.15.cloned.1.call-update) | async-done | bytes 131088 | tf_op jit(solution)/shard_map/reduce_scatter | solution.py:220
  964.2 141.8 %reduce-scatter.17.cloned.1.call-done = f32[64,512]{1,0:T(8,128)} async-done(((f32[2048,512]{1,0:T(8,128)}), f32[64,512]{1,0:T(8,128)}) %reduce-scatter.17.cloned.1.call-update) | async-done | bytes 131088 | tf_op jit(solution)/shard_map/reduce_scatter | solution.py:221
  1109.0 6.5 add_add_fusion.2
  1115.4 36.8 %psum.7 = f32[]{:T(128)} all-reduce(f32[]{:T(128)S(6)} %add.259), channel_id=1, replica_groups=mesh['dp'=4,'seq'=8] {'dp','seq'}, use_global_device_ids=true, to_apply=%region_31.32 | all-reduce | flops 1 | bytes 8 | tf_op jit(solution)/shard_map/psum | solution.py:226
  (217 shorter events, 45.1 us)
Async XLA Ops:
  7.2 82.8 %copy-start.57 = (s32[8]{0:T(128)S(1)}, s32[8]{0:T(128)}, u32[]{:S(2)}) copy-start(s32[8]{0:T(128)} %param.20) | copy-start | bytes 100
  7.2 80.5 %copy-start.1 = (bf16[8,256,512]{2,1,0:T(8,128)(2,1)S(1)}, bf16[8,256,512]{2,1,0:T(8,128)(2,1)}, u32[]{:S(2)}) copy-start(bf16[8,256,512]{2,1,0:T(8,128)(2,1)} %param.18) | copy-start | bytes 6291460
  7.2 83.0 %copy-start.36 = (f32[16,512]{1,0:T(8,128)S(1)}, f32[16,512]{1,0:T(8,128)}, u32[]{:S(2)}) copy-start(f32[16,512]{1,0:T(8,128)} %param.22) | copy-start | bytes 98308
  7.2 156.9 %all-gather.5.cloned.1.call-start = ((), (), s32[]{:S(2)}) async-start(), calls=%async_computation.6 | async-start | bytes 1622016 | tf_op jit(solution)/shard_map/all_gather | solution.py:68
  9.0 253.6 %all-gather.7.cloned.1.call-start = ((), (), s32[]{:S(2)}) async-start(), calls=%async_computation.7 | async-start | bytes 2162688 | tf_op jit(solution)/shard_map/all_gather | solution.py:70
  10.6 266.5 %all-gather.9.cloned.1.call-start = ((), (), s32[]{:S(2)}) async-start(), calls=%async_computation.8 | async-start | bytes 2162688 | tf_op jit(solution)/shard_map/all_gather | solution.py:71
  12.2 397.8 %reduce-scatter.9.cloned.1.call-start = ((), (), s32[]{:S(2)}) async-start(), calls=%async_computation.9 | async-start | bytes 589824 | tf_op jit(solution)/shard_map/reduce_scatter | solution.py:202
  85.7 78.4 %copy-start.47 = (f32[1,512]{1,0:T(1,128)}, f32[1,512]{1,0:T(1,128)S(1)}, u32[]{:S(2)}) copy-start(f32[1,512]{1,0:T(1,128)S(1)} %get-tuple-element.51) | copy-start | bytes 6148
  85.7 78.4 %copy-start.53 = (f32[1,512]{1,0:T(1,128)}, f32[1,512]{1,0:T(1,128)S(1)}, u32[]{:S(2)}) copy-start(f32[1,512]{1,0:T(1,128)S(1)} %get-tuple-element.50) | copy-start | bytes 6148
  87.7 84.6 %copy-start.40 = (f32[8,256]{1,0:T(8,128)}, f32[8,256]{1,0:T(8,128)S(1)}, u32[]{:S(2)}) copy-start(f32[8,256]{1,0:T(8,128)S(1)} %get-tuple-element.53) | copy-start | bytes 24580
  89.8 82.4 %copy-start.28 = (f32[2048]{0:T(1024)}, f32[2048]{0:T(1024)S(1)}, u32[]{:S(2)}) copy-start(f32[2048]{0:T(1024)S(1)} %rsqrt.23) | copy-start | bytes 24580
  89.8 82.4 %copy-start.30 = (f32[1,2,8,128]{3,1,2,0:T(2,128)}, f32[1,2,8,128]{3,1,2,0:T(2,128)S(1)}, u32[]{:S(2)}) copy-start(f32[1,2,8,128]{3,1,2,0:T(2,128)S(1)} %copy.221) | copy-start | bytes 24580
  199.5 37.3 %copy-start.10 = (bf16[8,2,128,1,8,64]{2,1,0,5,4,3:T(2,128)(2,1)S(1)}, bf16[8,2,128,1,8,64]{2,1,0,5,4,3:T(2,128)(2,1)}, u32[]{:S(2)}) copy-start(bf16[8,2,128,1,8,64]{2,1,0,5,4,3:T(2,128)(2,1)} %get-tuple-element.41) | copy-start | bytes 6291460
  199.5 37.3 %copy-start.12 = (bf16[8,2,128,1,8,64]{2,1,0,5,4,3:T(2,128)(2,1)S(1)}, bf16[8,2,128,1,8,64]{2,1,0,5,4,3:T(2,128)(2,1)}, u32[]{:S(2)}) copy-start(bf16[8,2,128,1,8,64]{2,1,0,5,4,3:T(2,128)(2,1)} %get-tuple-element.42) | copy-start | bytes 6291460
  277.1 20.3 %copy-start.3 = (f32[2048,512]{1,0:T(8,128)S(1)}, f32[2048,512]{1,0:T(8,128)}, u32[]{:S(2)}) copy-start(f32[2048,512]{1,0:T(8,128)} %copy-done.2) | copy-start | bytes 12582916
  277.1 20.3 %copy-start.45 = (f32[2048]{0:T(1024)S(1)}, f32[2048]{0:T(1024)}, u32[]{:S(2)}) copy-start(f32[2048]{0:T(1024)} %copy-done.44) | copy-start | bytes 24580
  277.1 20.3 %copy-start.51 = (f32[2048]{0:T(1024)S(1)}, f32[2048]{0:T(1024)}, u32[]{:S(2)}) copy-start(f32[2048]{0:T(1024)} %fusion.102) | copy-start | bytes 24580
  277.1 20.3 %copy-start.55 = (f32[1,512]{1,0:T(1,128)S(1)}, f32[1,512]{1,0:T(1,128)}, u32[]{:S(2)}) copy-start(f32[1,512]{1,0:T(1,128)} %get-tuple-element.48) | copy-start | bytes 6148
  277.1 20.3 %copy-start.61 = (bf16[512,2048]{1,0:T(8,128)(2,1)S(1)}, bf16[512,2048]{1,0:T(8,128)(2,1)}, u32[]{:S(2)}) copy-start(bf16[512,2048]{1,0:T(8,128)(2,1)} %all-gather.7.cloned.1.call-done) | copy-start | bytes 6291460
  322.3 13.4 %slice-start = ((s8[8388608]{0:T(1024)(128)(4,1)}), s8[4194304]{0:T(1024)(128)(4,1)S(1)}, s32[]{:S(2)}) async-start(s8[8388608]{0:T(1024)(128)(4,1)} %bitcast.213), calls=%async_computation.15 | async-start | bytes 8388608
  325.9 9.1 copy-start.7
  325.9 9.8 slice-start.1
  349.9 229.2 %reduce-scatter.19.cloned.1.call-start = ((), (), s32[]{:S(2)}) async-start(), calls=%async_computation.14 | async-start | bytes 270336
  354.6 55.4 %copy-start.50 = (f32[8,2,128]{2,1,0:T(2,128)S(1)}, f32[8,2,128]{2,1,0:T(2,128)}, u32[]{:S(2)}) copy-start(f32[8,2,128]{2,1,0:T(2,128)} %get-tuple-element.54) | copy-start | bytes 24580
  423.2 11.1 copy-start.31
  423.2 11.1 copy-start.48
  434.4 8.9 copy-start.29
  446.5 266.0 %reduce-scatter.13.cloned.1.call-start = ((), (), s32[]{:S(2)}) async-start(), calls=%async_computation.11 | async-start | bytes 1081344 | tf_op jit(solution)/shard_map/reduce_scatter | solution.py:219
  451.0 365.7 %reduce-scatter.11.cloned.1.call-start = ((), (), s32[]{:S(2)}) async-start(), calls=%async_computation.10 | async-start | bytes 3244032 | tf_op jit(solution)/shard_map/reduce_scatter | solution.py:218
  452.0 8.2 copy-start.46
  452.0 8.2 copy-start.52
  452.0 8.2 copy-start.56
  452.0 8.2 copy-start.58
  460.0 502.0 %reduce-scatter.15.cloned.1.call-start = ((), (), s32[]{:S(2)}) async-start(), calls=%async_computation.12 | async-start | bytes 4325376 | tf_op jit(solution)/shard_map/reduce_scatter | solution.py:220
  471.7 634.3 %reduce-scatter.17.cloned.1.call-start = ((), (), s32[]{:S(2)}) async-start(), calls=%async_computation.13 | async-start | bytes 4325376 | tf_op jit(solution)/shard_map/reduce_scatter | solution.py:221
  1108.8 45.5 %copy-start.22 = (f32[64,512]{1,0:T(8,128)S(1)}, f32[64,512]{1,0:T(8,128)}, u32[]{:S(2)}) copy-start(f32[64,512]{1,0:T(8,128)} %param.24) | copy-start | bytes 393220
  1108.8 45.5 %copy-start.25 = (f32[64,512]{1,0:T(8,128)S(1)}, f32[64,512]{1,0:T(8,128)}, u32[]{:S(2)}) copy-start(f32[64,512]{1,0:T(8,128)} %reduce-scatter.17.cloned.1.call-done) | copy-start | bytes 393220
  1108.8 45.5 %copy-start.32 = (f32[64,512]{1,0:T(8,128)S(1)}, f32[64,512]{1,0:T(8,128)}, u32[]{:S(2)}) copy-start(f32[64,512]{1,0:T(8,128)} %param.29) | copy-start | bytes 393220
  1108.9 45.5 %copy-start.33 = (f32[64,512]{1,0:T(8,128)S(1)}, f32[64,512]{1,0:T(8,128)}, u32[]{:S(2)}) copy-start(f32[64,512]{1,0:T(8,128)} %param.34) | copy-start | bytes 393220
  1108.9 46.3 %copy-start.23 = (f32[16,2048]{1,0:T(8,128)S(1)}, f32[16,2048]{1,0:T(8,128)}, u32[]{:S(2)}) copy-start(f32[16,2048]{1,0:T(8,128)} %param.23) | copy-start | bytes 393220
  1108.9 46.3 %copy-start.24 = (f32[16,2048]{1,0:T(8,128)S(1)}, f32[16,2048]{1,0:T(8,128)}, u32[]{:S(2)}) copy-start(f32[16,2048]{1,0:T(8,128)} %reduce-scatter.15.cloned.1.call-done) | copy-start | bytes 393220
  1108.9 46.2 %copy-start.34 = (f32[16,2048]{1,0:T(8,128)S(1)}, f32[16,2048]{1,0:T(8,128)}, u32[]{:S(2)}) copy-start(f32[16,2048]{1,0:T(8,128)} %param.28) | copy-start | bytes 393220
  1108.9 46.2 %copy-start.35 = (f32[16,2048]{1,0:T(8,128)S(1)}, f32[16,2048]{1,0:T(8,128)}, u32[]{:S(2)}) copy-start(f32[16,2048]{1,0:T(8,128)} %param.33) | copy-start | bytes 393220
  1108.9 47.0 %copy-start.37 = (f32[16,512]{1,0:T(8,128)S(1)}, f32[16,512]{1,0:T(8,128)}, u32[]{:S(2)}) copy-start(f32[16,512]{1,0:T(8,128)} %param.22) | copy-start | bytes 98308
  1108.9 47.0 %copy-start.38 = (f32[16,512]{1,0:T(8,128)S(1)}, f32[16,512]{1,0:T(8,128)}, u32[]{:S(2)}) copy-start(f32[16,512]{1,0:T(8,128)} %reduce-scatter.13.cloned.1.call-done) | copy-start | bytes 98308
  1108.9 48.5 %copy-start.26 = (f32[16,1536]{1,0:T(8,128)S(1)}, f32[16,1536]{1,0:T(8,128)}, u32[]{:S(2)}) copy-start(f32[16,1536]{1,0:T(8,128)} %param.21) | copy-start | bytes 294916
  1108.9 48.4 %copy-start.27 = (f32[16,1536]{1,0:T(8,128)S(1)}, f32[16,1536]{1,0:T(8,128)}, u32[]{:S(2)}) copy-start(f32[16,1536]{1,0:T(8,128)} %reduce-scatter.11.cloned.1.call-done) | copy-start | bytes 294916
  1109.0 48.4 %copy-start.39 = (f32[16,1536]{1,0:T(8,128)S(1)}, f32[16,1536]{1,0:T(8,128)}, u32[]{:S(2)}) copy-start(f32[16,1536]{1,0:T(8,128)} %param.26) | copy-start | bytes 294916
  (26 other events, 84.7 us)
Sparse Core Ops, SparseCore 0:
  11.6 57.8 all-gather.4
  73.0 56.9 all-gather.6
  133.5 55.1 all-gather.8
  350.0 59.9 reduce-scatter.8
  446.5 132.5 reduce-scatter.18
  581.2 131.2 reduce-scatter.12
  718.8 97.8 reduce-scatter.10
  819.1 142.8 reduce-scatter.14
  964.4 141.5 reduce-scatter.16
where the time goes:
time: 1180 us; the launch traced here: 1170 us
  waiting for transfers between devices  655 us (56%)
  blocking collectives  210 us (18%)
  matrix products  153 us (13%)
  local copies, waits for them, and re-layouts  74.6 us (6%)
  other arithmetic  53.2 us (5%)
  between operations  20.1 us (2%)
    reduce_scatter x1, waiting for transfers between devices, per_device(): lax.psum_scatter(grad_up, ('dp', 'seq'), scatter_dimension=0, tiled=True)  142 us
    reduce_scatter x1, waiting for transfers between devices, per_device(): lax.psum_scatter(grad_down, ('dp', 'seq'), scatter_dimension=0, tiled=True)  142 us
    reduce_scatter x1, waiting for transfers between devices, per_device(): lax.psum_scatter(grad_out_proj, ('dp', 'seq'), scatter_dimension=0, tiled...  132 us
    reduce_scatter x1, waiting for transfers between devices, per_device(): lax.psum_scatter(grad_qkv, ('dp', 'seq'), scatter_dimension=0, tiled=True)  103 us
    unnamed x10, waiting for transfers between devices  85.9 us
    all_gather x1, blocking collectives, per_device(): lax.all_gather(w_out.astype(jnp.bfloat16), ('dp', 'seq'), axis=0, tiled=T...  72 us
    all_gather x1, blocking collectives, per_device(): lax.all_gather(norm_params.astype(jnp.bfloat16), ('dp', 'seq'), axis=1, t...  69.7 us
    reduce_scatter x1, waiting for transfers between devices, per_device(): lax.psum_scatter(pool_grads.astype(jnp.bfloat16), 'seq', scatter_dimensio...  50.4 us
  transfers between devices with their start and end apart: 9, of which 6 were waited for; matrix products, arithmetic and copies ran while one was open for 13% of the time, Pallas kernels for 0%

commit v1 on v0

--- a/solution.py
+++ b/solution.py
@@ -1,12 +1,18 @@
+import functools
+import math
+
 import jax
 import jax.numpy as jnp
 from jax import lax
+from jax.experimental import pallas as pl
+from jax.experimental.pallas import tpu as pltpu
 from jax.sharding import PartitionSpec as P
 
 HEADS = 8
 HEAD_DIM = 64
 SPAN = 128
 STEP = 10
+WIDTH = 512
 
 
 eps_norm = 1e-05
@@ -38,7 +44,7 @@
     return (weight_new, first_new, second_new)
 
 
-def per_device(
+def generic_device(
     tokens,
     cotangent,
     lengths,
@@ -263,6 +269,775 @@
     )
 
 
+BF = jnp.bfloat16
+F32 = jnp.float32
+MESH = pl.DeviceIdType.MESH
+LANES = 128
+TILE = 512
+NN = (((1,), (0,)), ((), ()))
+NT = (((1,), (1,)), ((), ()))
+TN = (((0,), (0,)), ((), ()))
+GATHER, REDUCE, POOL, POOLBACK, SQUARES, COPIES = 0, 24, 48, 55, 62, 72
+
+
+def mm(left, right, dims=NN):
+    return lax.dot_general(left, right, dims, preferred_element_type=F32)
+
+
+def centered(values_in):
+    center = values_in - jnp.mean(values_in, axis=-1, keepdims=True)
+    scale = lax.rsqrt(jnp.mean(center * center, axis=-1, keepdims=True) + eps_norm)
+    return center * scale, scale
+
+
+def norm_back(grad_hat, hat, scale):
+    mean_grad = jnp.mean(grad_hat, axis=-1, keepdims=True)
+    mean_both = jnp.mean(grad_hat * hat, axis=-1, keepdims=True)
+    return scale * (grad_hat - mean_grad - hat * mean_both)
+
+
+def fold_rows(values_in):
+    rows, width = values_in.shape
+    return jnp.sum(values_in.reshape(rows // 8, 8, width), axis=0)
+
+
+def layer_kernel(
+    len_ref, x_any, dy_any, wq_ref, wo_ref, wu_ref, wd_ref, nrm_ref,
+    fq_ref, fo_ref, fu_ref, fd_ref, sq_ref, so_ref, su_ref, sd_ref,
+    act_any, dx_any, gn_ref,
+    nq_ref, nfq_ref, nsq_ref, no_ref, nfo_ref, nso_ref,
+    nu_ref, nfu_ref, nsu_ref, nd_ref, nfd_ref, nsd_ref, nnrm_ref,
+    bq, bu, bd, qkv, mix, prob, gq, gu, gdt, gd,
+    r1q, r2aq, r2bq, r3aq, r3bq, r4q,
+    r1u, s2au, s2bu, r2au, r2bu, r3au, r3bu, s3u, r4u,
+    r1d, s2ad, s2bd, r2ad, r2bd, r3ad, r3bd, s3d, r4d,
+    pool_all, pool_far, pool_grad, pool_send, pool_recv, spread,
+    nrow, nacc, act_s, dup_s, h_s, ht_s, dyt_s, dh_s, fin_q, fin_u, fin_d,
+    psq, psd, x_ref, dy_ref, dx_ref, send_sem, recv_sem, local_sem,
+):
+    ny, nc, nz, nx, blk, _ = bq.shape
+    dblk = bd.shape[4]
+    rows_all, width = x_ref.shape
+    width3 = 3 * width
+    ff = wu_ref.shape[1]
+    seq_n = nz * nx
+    dp_n = ny * nc
+    local_len = rows_all // len_ref.shape[0]
+    spans_here = local_len // SPAN
+    blocks = rows_all // SPAN
+    spans_all = spans_here * seq_n
+    tiles = rows_all // TILE
+    per_tile = TILE // SPAN
+    pairs = width // LANES
+    dp_i = lax.axis_index("dp")
+    sq_i = lax.axis_index("seq")
+    y, c = dp_i // nc, dp_i % nc
+    z, x = sq_i // nx, sq_i % nx
+
+    def dev(yy, cc, zz, xx):
+        return (yy * nc + cc, zz * nx + xx)
+
+    twin = dev(y, 1 - c, z, x)
+    over_x = dev(y, c, z, 1 - x)
+    over_y = dev(1 - y, c, z, x)
+
+    def hop(src, dst, index, target):
+        return pltpu.make_async_remote_copy(
+            src_ref=src, dst_ref=dst, send_sem=send_sem.at[index],
+            recv_sem=recv_sem.at[index], device_id=target, device_id_type=MESH,
+        )
+
+    load_x = pltpu.make_async_copy(x_any, x_ref, local_sem.at[0])
+    load_dy = pltpu.make_async_copy(dy_any, dy_ref, local_sem.at[1])
+    keep_act = pltpu.make_async_copy(dy_ref, act_any, local_sem.at[2])
+    keep_dx = pltpu.make_async_copy(dx_ref, dx_any, local_sem.at[3])
+    load_x.start()
+    load_dy.start()
+
+    barrier = pltpu.get_barrier_semaphore()
+    for step in range(1, seq_n):
+        pl.semaphore_signal(
+            barrier, inc=1, device_id=(dp_i, lax.rem(sq_i + step, seq_n)), device_id_type=MESH
+        )
+    for step in range(1, dp_n):
+        pl.semaphore_signal(
+            barrier, inc=1, device_id=(lax.rem(dp_i + step, dp_n), sq_i), device_id_type=MESH
+        )
+    pl.semaphore_wait(barrier, seq_n + dp_n - 2)
+
+    bq[y, c, z, x, :, 0:width3] = wq_ref[...].astype(BF)
+    bq[y, c, z, x, :, width3:] = nrm_ref[0:blk, :].astype(BF)
+    bu[y, c, z, x, :, 0:ff] = wu_ref[...].astype(BF)
+    bu[y, c, z, x, :, ff:] = wo_ref[...].astype(BF)
+    bd[y, c, z, x] = wd_ref[...].astype(BF)
+
+    def gather_hops(full, base):
+        cut = (full.shape[5] // 2) // LANES * LANES
+        one, two = pl.ds(0, cut), pl.ds(cut, full.shape[5] - cut)
+
+        def same(part, index, target):
+            return hop(part, part, base + index, target)
+
+        first = [
+            same(full.at[y, c, z, x], step - 1, dev(y, c, lax.rem(z + step, nz), x))
+            for step in range(1, nz)
+        ]
+        second = [
+            same(full.at[y, c, :, x, :, one], 3, over_x),
+            same(full.at[y, c, :, x, :, two], 4, over_y),
+        ]
+        third = [
+            same(full.at[y, c, :, :, :, one], 5, over_y),
+            same(full.at[:, c, :, x, :, two], 6, over_x),
+        ]
+        last = [same(full.at[:, c], 7, twin)]
+        return first, second, third, last
+
+    def start(hops):
+        for one in hops:
+            one.start()
+
+    def arrived(hops):
+        for one in hops:
+            one.wait_recv()
+
+    def sent(hops):
+        for one in hops:
+            one.wait_send()
+
+    hops_q = gather_hops(bq, GATHER)
+    hops_u = gather_hops(bu, GATHER + 8)
+    hops_d = gather_hops(bd, GATHER + 16)
+    start(hops_q[0])
+    start(hops_u[0])
+    start(hops_d[0])
+
+    def clear(index, carry):
+        gq[...] = jnp.zeros_like(gq)
+        gu[...] = jnp.zeros_like(gu)
+        gdt[...] = jnp.zeros_like(gdt)
+        return carry
+
+    lax.fori_loop(0, 1, clear, 0)
+    nacc[...] = jnp.zeros_like(nacc)
+    pool_grad[...] = jnp.zeros_like(pool_grad)
+
+    load_x.wait()
+    arrived(hops_q[0])
+    start(hops_q[1])
+    arrived(hops_q[1])
+    start(hops_q[2])
+    arrived(hops_q[2])
+    start(hops_q[3])
+    arrived(hops_u[0])
+    start(hops_u[1])
+    arrived(hops_d[0])
+    start(hops_d[1])
+    arrived(hops_q[3])
+
+    norm_cols = bq[:, :, :, :, :, width3:].reshape(width, LANES).astype(F32)
+    nrow[...] = norm_cols.T[0:8]
+
+    def w_qkv(lo, hi):
+        return bq[:, :, :, :, :, lo:hi].reshape(width, hi - lo)
+
+    def qkv_tile(tile, pooled):
+        rows = pl.ds(pl.multiple_of(tile * TILE, TILE), TILE)
+        hat, _ = centered(x_ref[rows, :].astype(F32))
+        h1 = (hat * nrow[0:1, :] + nrow[1:2, :]).astype(BF)
+        for part in range(3):
+            cols = pl.ds(part * width, width)
+            qkv[rows, cols] = mm(h1, w_qkv(part * width, (part + 1) * width)).astype(BF)
+        block_at = lax.broadcasted_iota(jnp.int32, (blocks, TILE), 0)
+        row_at = lax.broadcasted_iota(jnp.int32, (blocks, TILE), 1) + tile * TILE
+        pos = sq_i * local_len + lax.rem(row_at, local_len)
+        item = row_at // local_len
+        length = jnp.zeros((blocks, TILE), jnp.int32)
+        for i in range(TILE // local_len):
+            at = tile * (TILE // local_len) + i
+            length = jnp.where(item == at, len_ref[at], length)
+        pick = jnp.where((row_at // SPAN == block_at) & (pos < length), 1.0, 0.0).astype(BF)
+
+        @pl.when(tile == 1)
+        def _():
+            arrived(hops_u[1])
+            start(hops_u[2])
+
+        @pl.when(tile == 2)
+        def _():
+            arrived(hops_d[1])
+            start(hops_d[2])
+
+        return pooled + mm(pick, qkv[rows, width:])
+
+    pooled = lax.fori_loop(0, tiles, qkv_tile, jnp.zeros((blocks, 2 * width), F32))
+    block_col = lax.broadcasted_iota(jnp.int32, (blocks, 1), 0)
+    length_col = jnp.zeros((blocks, 1), jnp.int32)
+    for i in range(blocks // spans_here):
+        length_col = jnp.where(block_col // spans_here == i, len_ref[i], length_col)
+    first_pos = sq_i * local_len + lax.rem(block_col, spans_here) * SPAN
+    count_col = jnp.clip(length_col - first_pos, 1, SPAN).astype(F32)
+    pool_all[sq_i] = (pooled / count_col).astype(BF)
+    pool_hops = [
+        hop(
+            pool_all.at[sq_i], pool_all.at[sq_i], POOL + step - 1,
+            (dp_i, lax.rem(sq_i + step, seq_n)),
+        )
+        for step in range(1, seq_n)
+    ]
+    start(pool_hops)
+    arrived(hops_u[2])
+    start(hops_u[3])
+    arrived(hops_d[2])
+    start(hops_d[3])
+    arrived(pool_hops)
+
+    far_n = seq_n * blocks
+    to_row = lax.broadcasted_iota(jnp.int32, (far_n, far_n), 0)
+    to_col = lax.broadcasted_iota(jnp.int32, (far_n, far_n), 1)
+    item_row, span_row = to_row // spans_all, to_row % spans_all
+    wanted = (span_row // spans_here) * blocks + item_row * spans_here + span_row % spans_here
+    order = jnp.where(wanted == to_col, 1.0, 0.0).astype(BF)
+    pool_far[...] = mm(order, pool_all[...].reshape(far_n, 2 * width)).astype(BF)
+
+    keys_n = SPAN + spans_all
+    lane = lax.broadcasted_iota(jnp.int32, (1, LANES), 1)
+    score_scale = HEAD_DIM ** (-0.5)
+    half_a = jnp.where(lane < HEAD_DIM, 1.0, 0.0)
+    half_b = jnp.where(lane >= HEAD_DIM, 1.0, 0.0)
+    query_a, query_b = (half_a * score_scale).astype(BF), (half_b * score_scale).astype(BF)
+    grad_a, grad_b = half_a.astype(BF), half_b.astype(BF)
+
+    def both(near_rows, far_rows, cols):
+        return jnp.concatenate([qkv[near_rows, cols], pool_far[far_rows, cols_far(cols)]], axis=0)
+
+    def cols_far(cols):
+        return pl.ds(cols.start - width, cols.size)
+
+    def diagonal(stacked):
+        return jnp.concatenate(
+            [stacked[0:HEAD_DIM, 0:SPAN], stacked[HEAD_DIM:, SPAN:]], axis=0
+        ).T
+
+    def attend(block, carry):
+        item = block // spans_here
+        sub = lax.rem(block, spans_here)
+        rows = pl.ds(pl.multiple_of(block * SPAN, SPAN), SPAN)
+        far_rows = pl.ds(pl.multiple_of(item * spans_all, spans_all), spans_all)
+        length = len_ref[item]
+        key_at = lax.broadcasted_iota(jnp.int32, (keys_n, 2 * SPAN), 0)
+        span_at = key_at - SPAN
+        mine = sq_i * spans_here + sub
+        near_ok = (key_at < SPAN) & (mine * SPAN + key_at < length)
+        far_ok = (key_at >= SPAN) & (span_at * SPAN < length) & (span_at != mine)
+        seen = near_ok | far_ok
+        for pair in range(pairs):
+            q2 = qkv[rows, pl.ds(pair * LANES, LANES)]
+            kk = both(rows, far_rows, pl.ds(width + pair * LANES, LANES))
+            vv = both(rows, far_rows, pl.ds(2 * width + pair * LANES, LANES))
+            qq = jnp.concatenate([q2 * query_a, q2 * query_b], axis=0)
+            score = jnp.where(seen, mm(kk, qq, NT), neg_fill)
+            top = jnp.max(score, axis=0, keepdims=True)
+            raised = jnp.exp(score - top)
+            share = (raised * (1.0 / jnp.sum(raised, axis=0, keepdims=True))).astype(BF)
+            prob[block, pair] = share
+            mixed = diagonal(mm(vv, share, TN))
+            mix[rows, pl.ds(pair * LANES, LANES)] = mixed.astype(BF)
+        return carry
+
+    lax.fori_loop(0, blocks, attend, 0)
+    arrived(hops_u[3])
+    arrived(hops_d[3])
+    for hops in (hops_q, hops_u, hops_d):
+        for group in hops:
+            sent(group)
+    sent(pool_hops)
+
+    load_dy.wait()
+    w_out = bu[:, :, :, :, :, ff:].reshape(width, width)
+    gelu_in = math.sqrt(2.0 / math.pi)
+    gelu_cube = 0.044715
+
+    tall_tile = (nz, nx, dblk, width)
+    half_tile = TILE // 2
+
+    def ffn_tile(tile, carry):
+        rows = pl.ds(pl.multiple_of(tile * TILE, TILE), TILE)
+        x1 = x_ref[rows, :].astype(F32) + mm(mix[rows, :], w_out)
+        hat, scale = centered(x1)
+        gd[0] = x1.reshape(tall_tile)
+        gd[1] = hat.reshape(tall_tile)
+        h2 = hat * nrow[2:3, :] + nrow[3:4, :]
+        h_s[...] = h2.astype(BF)
+        ht_s[...] = h2.T.astype(BF)
+        dyt_s[...] = dy_ref[rows, :].astype(F32).T.astype(BF)
+        dh_s[...] = jnp.zeros_like(dh_s)
+
+        def ffn_part(part, inner):
+            cols = pl.ds(pl.multiple_of(part * TILE, TILE), TILE)
+            w_up = bu[:, :, :, :, :, cols].reshape(width, TILE)
+            w_down = bd[part // nc, part % nc].reshape(TILE, width)
+            for part_rows in range(2):
+                some = pl.ds(part_rows * half_tile, half_tile)
+                up = mm(h_s[some, :], w_up)
+                square = up * up
+                bent = jnp.tanh(up * (gelu_in + (gelu_in * gelu_cube) * square))
+                half = 0.5 + 0.5 * bent
+                act_s[some, :] = (up * half).astype(BF)
+                rate = half + (up * (1.0 - bent * bent)) * (
+                    0.5 * gelu_in + (1.5 * gelu_in * gelu_cube) * square
+                )
+                near = pl.ds(pl.multiple_of(tile * TILE + part_rows * half_tile, half_tile), half_tile)
+                dup_s[some, :] = (mm(dy_ref[near, :], w_down, NT) * rate).astype(BF)
+            gd[0] += mm(act_s[...], w_down).reshape(tall_tile)
+            gdt[:, cols] += mm(dyt_s[...], act_s[...])
+            gu[:, :, :, :, :, cols] += mm(ht_s[...], dup_s[...]).reshape(
+                ny, nc, nz, nx, blk, TILE
+            )
+            dh_s[...] += mm(dup_s[...], w_up, NT)
+            return inner
+
+        lax.fori_loop(0, ff // TILE, ffn_part, 0)
+        dh2 = dh_s[...]
+        hat = gd[1].reshape(TILE, width)
+        nacc[2] += fold_rows(dh2 * hat)
+        nacc[3] += fold_rows(dh2)
+        dx1 = dy_ref[rows, :].astype(F32) + norm_back(dh2 * nrow[2:3, :], hat, scale)
+        dy_ref[rows, :] = gd[0].reshape(TILE, width).astype(BF)
+        dx_ref[rows, :] = dx1
+        dz = dx1.astype(BF)
+        gu[:, :, :, :, :, ff:] += mm(mix[rows, :], dz, TN).reshape(ny, nc, nz, nx, blk, width)
+        mix[rows, :] = mm(dz, w_out, NT).astype(BF)
+        return carry
+
+    lax.fori_loop(0, tiles, ffn_tile, 0)
+    keep_act.start()
+
+    def each(count, body):
+        def step(index, carry):
+            body(index)
+            return carry
+
+        lax.fori_loop(0, count, step, 0)
+
+    def reduce_steps(own, load_other, s1, r1, s2a, s2b, r2a, r2b, r3a, r3b, s3, r4, fin, base):
+        n = s1.shape[4]
+        cut = (n // 2) // LANES * LANES
+        one, two = pl.ds(0, cut), pl.ds(cut, n - cut)
+        hop1 = [hop(s1, r1, base, twin)]
+        hop2 = [
+            hop(s1.at[1 - y, :, :, :, one], r2a, base + 1, over_y),
+            hop(s1.at[:, :, 1 - x, :, two], r2b, base + 2, over_x),
+        ]
+        hop3 = [
+            hop(s2a.at[:, 1 - x], r3a, base + 3, over_x),
+            hop(s2b.at[1 - y], r3b, base + 4, over_y),
+        ]
+        hop4 = [
+            hop(
+                s3.at[lax.rem(z + step, nz)], r4.at[step - 1], base + 4 + step,
+                dev(y, c, lax.rem(z + step, nz), x),
+            )
+            for step in range(1, nz)
+        ]
+
+        def stage1():
+            load_other()
+            start(hop1)
+
+        def stage2():
+            arrived(hop1)
+            sent(hop1)
+
+            def add(index):
+                yy, zz, xx = index // (nz * nx), (index // nx) % nz, index % nx
+                total = own[yy, zz, xx] + r1[yy, zz, xx].astype(F32)
+                own[yy, zz, xx] = total
+                s1[yy, zz, xx] = total.astype(BF)
+
+            each(ny * nz * nx, add)
+            start(hop2)
+
+        def stage3():
+            arrived(hop2)
+            for zz in range(nz):
+                for xx in range(nx):
+                    total = own[y, zz, xx, :, one] + r2a[zz, xx].astype(F32)
+                    own[y, zz, xx, :, one] = total
+                    s2a[zz, xx] = total.astype(BF)
+            hop3[0].start()
+            for yy in range(ny):
+                for zz in range(nz):
+                    total = own[yy, zz, x, :, two] + r2b[yy, zz].astype(F32)
+                    own[yy, zz, x, :, two] = total
+                    s2b[yy, zz] = total.astype(BF)
+            hop3[1].start()
+
+        def stage4():
+            arrived(hop3)
+            for zz in range(nz):
+                total = own[y, zz, x, :, one] + r3a[zz].astype(F32)
+                own[y, zz, x, :, one] = total
+                s3[zz, :, one] = total.astype(BF)
+                total = own[y, zz, x, :, two] + r3b[zz].astype(F32)
+                own[y, zz, x, :, two] = total
+                s3[zz, :, two] = total.astype(BF)
+            start(hop4)
+
+        def stage5():
+            arrived(hop4)
+            total = own[y, z, x]
+            for step in range(nz - 1):
+                total = total + r4[step].astype(F32)
+            fin[...] = total
+            sent(hop2)
+            sent(hop3)
+            sent(hop4)
+
+        return stage1, stage2, stage3, stage4, stage5
+
+    def plain_own(full):
+        return full.at[:, c]
+
+    def plain_other(full, s1):
+        def load():
+            def one(index):
+                yy, zz, xx = index // (nz * nx), (index // nx) % nz, index % nx
+                s1[yy, zz, xx] = full[yy, 1 - c, zz, xx].astype(BF)
+
+            each(ny * nz * nx, one)
+
+        return load
+
+    def down_other():
+        group = nz * nx * dblk
+        for yy in range(ny):
+            for cc, is_own in ((c, True), (1 - c, False)):
+                for part in range(group // LANES):
+                    at = pl.multiple_of((yy * nc + cc) * group + part * LANES, LANES)
+                    piece = gdt[:, pl.ds(at, LANES)].T.reshape(LANES // dblk, dblk, width)
+                    for inner in range(LANES // dblk):
+                        where = part * (LANES // dblk) + inner
+                        if is_own:
+                            gd[yy, where // nx, where % nx] = piece[inner]
+                        else:
+                            s1d[yy, where // nx, where % nx] = piece[inner].astype(BF)
+
+    s1u, s1d = bu.at[:, 0], bd.at[:, 0]
+    cols_q = r1q.shape[4]
+    cut_q = r3aq.shape[2]
+    s1q = bu.at[:, 1, :, :, :, pl.ds(0, cols_q)]
+    s2aq = s2au.at[:, :, :, pl.ds(0, cut_q)]
+    s2bq = s2bu.at[:, :, :, pl.ds(0, cols_q - cut_q)]
+    s3q = s3u.at[:, :, pl.ds(0, cols_q)]
+    red_d = reduce_steps(
+        gd, down_other, s1d, r1d, s2ad, s2bd, r2ad, r2bd, r3ad, r3bd, s3d, r4d, fin_d, REDUCE
+    )
+    red_u = reduce_steps(
+        plain_own(gu), plain_other(gu, s1u), s1u, r1u, s2au, s2bu, r2au, r2bu, r3au, r3bu,
+        s3u, r4u, fin_u, REDUCE + 8,
+    )
+    red_q = reduce_steps(
+        plain_own(gq), plain_other(gq, s1q), s1q, r1q, s2aq, s2bq, r2aq, r2bq, r3aq, r3bq,
+        s3q, r4q, fin_q, REDUCE + 16,
+    )
+    red_d[0]()
+    red_u[0]()
+
+    def attend_back(block, carry):
+        for at, steps in ((1, 1), (5, 2), (10, 3)):
+
+            @pl.when(block == at)
+            def _(steps=steps):
+                red_d[steps]()
+                red_u[steps]()
+
+        item = block // spans_here
+        rows = pl.ds(pl.multiple_of(block * SPAN, SPAN), SPAN)
+        far_rows = pl.ds(pl.multiple_of(item * spans_all, spans_all), spans_all)
+        for pair in range(pairs):
+            q_cols = pl.ds(pair * LANES, LANES)
+            k_cols = pl.ds(width + pair * LANES, LANES)
+            v_cols = pl.ds(2 * width + pair * LANES, LANES)
+            q2 = qkv[rows, q_cols]
+            do2 = mix[rows, q_cols]
+            kk = both(rows, far_rows, k_cols)
+            vv = both(rows, far_rows, v_cols)
+            qq = jnp.concatenate([q2 * query_a, q2 * query_b], axis=0)
+            dd = jnp.concatenate([do2 * grad_a, do2 * grad_b], axis=0)
+            share = prob[block, pair]
+            share_f = share.astype(F32)
+            dshare = mm(vv, dd, NT)
+            inner = jnp.sum(share_f * dshare, axis=0, keepdims=True)
+            dscore = (share_f * (dshare - inner)).astype(BF)
+            dq = diagonal(mm(kk, dscore, TN)) * score_scale
+            dk = mm(dscore, qq)
+            dv = mm(share, dd)
+            qkv[rows, q_cols] = dq.astype(BF)
+            qkv[rows, k_cols] = dk[0:SPAN].astype(BF)
+            qkv[rows, v_cols] = dv[0:SPAN].astype(BF)
+            pool_grad[far_rows, q_cols] += dk[SPAN:]
+            pool_grad[far_rows, pl.ds(width + pair * LANES, LANES)] += dv[SPAN:]
+        return carry
+
+    lax.fori_loop(0, blocks, attend_back, 0)
+
+    back_row = lax.broadcasted_iota(jnp.int32, (far_n, far_n), 0)
+    back_col = lax.broadcasted_iota(jnp.int32, (far_n, far_n), 1)
+    owner, place = back_row // blocks, back_row % blocks
+    source = (place // spans_here) * spans_all + owner * spans_here + place % spans_here
+    reorder = jnp.where(source == back_col, 1.0, 0.0).astype(BF)
+    pool_send[...] = (
+        mm(reorder, pool_grad[...].astype(BF)).astype(BF).reshape(seq_n, blocks, 2 * width)
+    )
+    back_hops = [
+        hop(
+            pool_send.at[lax.rem(sq_i + step, seq_n)], pool_recv.at[step - 1],
+            POOLBACK + step - 1, (dp_i, lax.rem(sq_i + step, seq_n)),
+        )
+        for step in range(1, seq_n)
+    ]
+    start(back_hops)
+    arrived(back_hops)
+    pool_total = pool_send[sq_i].astype(F32)
+    for step in range(seq_n - 1):
+        pool_total = pool_total + pool_recv[step].astype(F32)
+    spread[...] = pool_total / count_col
+
+    def last_tile(tile, carry):
+        rows = pl.ds(pl.multiple_of(tile * TILE, TILE), TILE)
+        hat, scale = centered(x_ref[rows, :].astype(F32))
+        h1 = (hat * nrow[0:1, :] + nrow[1:2, :]).astype(BF)
+        for part in range(per_tile):
+            block = tile * per_tile + part
+            own_rows = pl.ds(pl.multiple_of(block * SPAN, SPAN), SPAN)
+            pos = (
+                sq_i * local_len
+                + lax.rem(block, spans_here) * SPAN
+                + lax.broadcasted_iota(jnp.int32, (SPAN, 1), 0)
+            )
+            live = jnp.where(pos < len_ref[block // spans_here], 1.0, 0.0)
+            far = live * spread[pl.ds(block, 1), :]
+            qkv[own_rows, width:] = (qkv[own_rows, width:].astype(F32) + far).astype(BF)
+        ht_s[...] = h1.astype(F32).T.astype(BF)
+        dh_s[...] = jnp.zeros_like(dh_s)
+        for part in range(3):
+            cols = pl.ds(part * width, width)
+            gq[:, :, :, :, :, cols] += mm(ht_s[...], qkv[rows, cols]).reshape(
+                ny, nc, nz, nx, blk, width
+            )
+            dh_s[...] += mm(qkv[rows, cols], w_qkv(part * width, (part + 1) * width), NT)
+        dh1 = dh_s[...]
+        nacc[0] += fold_rows(dh1 * hat)
+        nacc[1] += fold_rows(dh1)
+        dx_ref[rows, :] += norm_back(dh1 * nrow[0:1, :], hat, scale)
+        return carry
+
+    lax.fori_loop(0, tiles, last_tile, 0)
+    keep_dx.start()
+    norm_rows = [jnp.sum(nacc[k], axis=0, keepdims=True) for k in range(4)]
+    norm_rows.append(jnp.zeros((LANES - 4, width), F32))
+    gq[:, :, :, :, :, width3:] = (
+        jnp.concatenate(norm_rows, axis=0).T.reshape(ny, nc, nz, nx, blk, LANES)
+    )
+    red_q[0]()
+    red_d[4]()
+    red_u[4]()
+    red_q[1]()
+    red_q[2]()
+    red_q[3]()
+    sent(back_hops)
+    red_q[4]()
+
+    def partial(ref):
+        values_in = ref[...]
+        squares = fold_rows(values_in * values_in)
+        return sum(
+            squares[:, k * LANES : (k + 1) * LANES] for k in range(squares.shape[1] // LANES)
+        )
+
+    psq[sq_i] = partial(fin_q) + partial(fin_u) + partial(fin_d)
+    seq_hops = [
+        hop(
+            psq.at[sq_i], psq.at[sq_i], SQUARES + step - 1,
+            (dp_i, lax.rem(sq_i + step, seq_n)),
+        )
+        for step in range(1, seq_n)
+    ]
+    start(seq_hops)
+    arrived(seq_hops)
+    total = psq[0]
+    for k in range(1, seq_n):
+        total = total + psq[k]
+    psd[dp_i] = total
+    dp_hops = [
+        hop(
+            psd.at[dp_i], psd.at[dp_i], SQUARES + seq_n - 2 + step,
+            (lax.rem(dp_i + step, dp_n), sq_i),
+        )
+        for step in range(1, dp_n)
+    ]
+    start(dp_hops)
+    arrived(dp_hops)
+    total = psd[0]
+    for k in range(1, dp_n):
+        total = total + psd[k]
+    grad_norm = jnp.sqrt(jnp.sum(jnp.sum(total, axis=1, keepdims=True), axis=0, keepdims=True))
+    factor = clip_bound / jnp.maximum(grad_norm, clip_bound)
+    gn_ref[...] = jnp.broadcast_to(grad_norm, gn_ref.shape)
+
+    def update(weight, grad_in, first, second, outs, rate, decay):
+        new = adamw_update(weight, grad_in, first, second, factor, rate, decay)
+        for out, value in zip(outs, new):
+            out[...] = value
+
+    update(
+        wq_ref[...], fin_q[:, 0:width3], fq_ref[...], sq_ref[...],
+        (nq_ref, nfq_ref, nsq_ref), rate_matrix, decay_coef,
+    )
+    update(
+        wo_ref[...], fin_u[:, ff:], fo_ref[...], so_ref[...],
+        (no_ref, nfo_ref, nso_ref), rate_matrix, decay_coef,
+    )
+    update(
+        wu_ref[...], fin_u[:, 0:ff], fu_ref[...], su_ref[...],
+        (nu_ref, nfu_ref, nsu_ref), rate_matrix, decay_coef,
+    )
+    update(
+        wd_ref[...], fin_d[...], fd_ref[...], sd_ref[...],
+        (nd_ref, nfd_ref, nsd_ref), rate_matrix, decay_coef,
+    )
+    update(
+        nrm_ref[0:blk, :], fin_q[:, width3:], nrm_ref[blk : 2 * blk, :],
+        nrm_ref[2 * blk :, :],
+        (
+            nnrm_ref.at[pl.ds(0, blk)],
+            nnrm_ref.at[pl.ds(blk, blk)],
+            nnrm_ref.at[pl.ds(2 * blk, blk)],
+        ),
+        rate_norm, 0.0,
+    )
+    sent(seq_hops)
+    sent(dp_hops)
+    keep_act.wait()
+    keep_dx.wait()
+
+
+def fused_device(
+    tokens, cotangent, lengths, w_qkv, w_out, w_up, w_down, norm_params,
+    first_qkv, first_out, first_up, first_down, first_norm,
+    second_qkv, second_out, second_up, second_down, second_norm,
+):
+    item_count, local_len, width = tokens.shape
+    rows_all = item_count * local_len
+    dp_n, seq_n = lax.axis_size("dp"), lax.axis_size("seq")
+    nc = 2
+    ny = dp_n // nc
+    nx = ny
+    nz = seq_n // nx
+    blk, width3 = w_qkv.shape
+    ff = w_up.shape[1]
+    dblk = w_down.shape[0]
+    blocks = rows_all // SPAN
+    far_n = seq_n * blocks
+    keys_n = SPAN + local_len // SPAN * seq_n
+
+    def tall(rows_in):
+        return jnp.pad(rows_in.T, ((0, 0), (0, LANES - rows_in.shape[0])))
+
+    norm_pack = jnp.concatenate([tall(norm_params), tall(first_norm), tall(second_norm)], axis=0)
+    matrices = (w_qkv, w_out, w_up, w_down)
+    triples = [jax.ShapeDtypeStruct(w.shape, F32) for w in matrices for _ in range(3)]
+    nq, nu, nd = width3 + LANES, ff + width, width
+
+    def bufs(b, n, sends):
+        cut = (n // 2) // LANES * LANES
+        rest = n - cut
+        taken = [pltpu.VMEM((nz, nx, b, cut), BF), pltpu.VMEM((ny, nz, b, rest), BF)]
+        return [
+            pltpu.VMEM((ny, nz, nx, b, n), BF),
+            *(taken if sends else []),
+            *taken,
+            pltpu.VMEM((nz, b, cut), BF),
+            pltpu.VMEM((nz, b, rest), BF),
+            *([pltpu.VMEM((nz, b, n), BF)] if sends else []),
+            pltpu.VMEM((nz - 1, b, n), BF),
+        ]
+
+    whole = pl.BlockSpec(memory_space=pltpu.VMEM)
+    outside = pl.BlockSpec(memory_space=pl.ANY)
+    outs = pl.pallas_call(
+        layer_kernel,
+        out_shape=[
+            jax.ShapeDtypeStruct((rows_all, width), BF),
+            jax.ShapeDtypeStruct((rows_all, width), F32),
+            jax.ShapeDtypeStruct((8, LANES), F32),
+            *triples,
+            jax.ShapeDtypeStruct(norm_pack.shape, F32),
+        ],
+        in_specs=[pl.BlockSpec(memory_space=pltpu.SMEM), outside, outside] + [whole] * 13,
+        out_specs=[outside, outside] + [whole] * 14,
+        scratch_shapes=[
+            pltpu.VMEM((ny, nc, nz, nx, blk, nq), BF),
+            pltpu.VMEM((ny, nc, nz, nx, blk, nu), BF),
+            pltpu.VMEM((ny, nc, nz, nx, dblk, nd), BF),
+            pltpu.VMEM((rows_all, width3), BF),
+            pltpu.VMEM((rows_all, width), BF),
+            pltpu.VMEM((blocks, width // LANES, keys_n, 2 * SPAN), BF),
+            pltpu.VMEM((ny, nc, nz, nx, blk, nq), F32),
+            pltpu.VMEM((ny, nc, nz, nx, blk, nu), F32),
+            pltpu.VMEM((width, ff), F32),
+            pltpu.VMEM((ny, nz, nx, dblk, nd), F32),
+            *bufs(blk, nq, False),
+            *bufs(blk, nu, True),
+            *bufs(dblk, nd, True),
+            pltpu.VMEM((seq_n, blocks, 2 * width), BF),
+            pltpu.VMEM((far_n, 2 * width), BF),
+            pltpu.VMEM((far_n, 2 * width), F32),
+            pltpu.VMEM((seq_n, blocks, 2 * width), BF),
+            pltpu.VMEM((seq_n - 1, blocks, 2 * width), BF),
+            pltpu.VMEM((blocks, 2 * width), F32),
+            pltpu.VMEM((8, width), F32),
+            pltpu.VMEM((4, 8, width), F32),
+            pltpu.VMEM((TILE, TILE), BF),
+            pltpu.VMEM((TILE, TILE), BF),
+            pltpu.VMEM((TILE, width), BF),
+            pltpu.VMEM((width, TILE), BF),
+            pltpu.VMEM((width, TILE), BF),
+            pltpu.VMEM((TILE, width), F32),
+            pltpu.VMEM((blk, nq), F32),
+            pltpu.VMEM((blk, nu), F32),
+            pltpu.VMEM((dblk, nd), F32),
+            pltpu.VMEM((seq_n, 8, LANES), F32),
+            pltpu.VMEM((dp_n, 8, LANES), F32),
+            pltpu.VMEM((rows_all, width), BF),
+            pltpu.VMEM((rows_all, width), BF),
+            pltpu.VMEM((rows_all, width), F32),
+            pltpu.SemaphoreType.DMA((COPIES,)),
+            pltpu.SemaphoreType.DMA((COPIES,)),
+            pltpu.SemaphoreType.DMA((4,)),
+        ],
+        compiler_params=pltpu.CompilerParams(
+            collective_id=0, has_side_effects=True, vmem_limit_bytes=64 * 1024 * 1024 - 65536
+        ),
+    )(
+        lengths,
+        tokens.reshape(rows_all, width),
+        cotangent.reshape(rows_all, width),
+        w_qkv, w_out, w_up, w_down, norm_pack,
+        first_qkv, first_out, first_up, first_down,
+        second_qkv, second_out, second_up, second_down,
+    )
+    act, grad, gnorm = outs[:3]
+    new_pack = outs[15]
+    count = norm_params.shape[0]
+    norms = [new_pack[k * blk : (k + 1) * blk, 0:count].T for k in range(3)]
+    return (
+        act.reshape(tokens.shape), grad.reshape(tokens.shape), gnorm[0, 0],
+        *outs[3:15], *norms,
+    )
+
+
 def solution(mesh):
     placed = (
         P("dp", "seq", None),
@@ -284,8 +1059,10 @@
         P(("dp", "seq"), None),
         P(None, ("dp", "seq")),
     )
+    dp_n, seq_n = mesh.shape["dp"], mesh.shape["seq"]
+    fits = dp_n == 4 and seq_n % 2 == 0 and WIDTH // (dp_n * seq_n) == 16
     return jax.shard_map(
-        per_device,
+        fused_device if fits else generic_device,
         mesh=mesh,
         in_specs=placed,
         out_specs=(

time: 1180 us -> 210 us (0.18); the launches traced: 1170 us -> 210 us
  waiting for transfers between devices: 655 us -> 0 us
  blocking collectives: 210 us -> 0 us
  Pallas kernels: 0 us -> 189 us
  matrix products: 153 us -> 0 us
  local copies, waits for them, and re-layouts: 74.6 us -> 19.1 us
  other arithmetic: 53.2 us -> 0.61 us
  between operations: 20.1 us -> 0.75 us
    reduce_scatter x5 -> x0, waiting for transfers between devices: 570 us -> none  [the longest x1 142 us: per_device(): lax.psum_scatter(grad_up, ('dp', 'seq'), scatter_dimension=0, tiled=True)]
    pallas_call x0 -> x1, Pallas kernels: none -> 189 us  [fused_device(): pl.pallas_call(layer_kernel, out_shape=[jax.ShapeDtypeStruct((rows_all, w...]
    all_gather x3 -> x0, blocking collectives: 173 us -> none  [the longest x1 72 us: per_device(): lax.all_gather(w_out.astype(jnp.bfloat16), ('dp', 'seq'), axis=0, tiled=T...]
    dot_general x25 -> x0, matrix products: 153 us -> none  [the longest x1 20.2 us: per_device(): jnp.dot(grad_out_b, full_down.T, preferred_element_type=jnp.float32)]
    unnamed x10 -> x0, waiting for transfers between devices: 85.9 us -> none
    convert_element_type x8 -> x0, local copies, waits for them, and re-layouts: 37.9 us -> none  [the longest x2 17.1 us: per_device(): grad_qkv_rows.reshape(row_count, 3 * model_width).astype(jnp.bfloat16)]
    psum x1 -> x0, blocking collectives: 36.8 us -> none  [per_device(): total_sq = lax.psum(squares, ('dp', 'seq'))]
    reduce_sum x14 -> x0, other arithmetic: 18.2 us -> none  [the longest x2 3.71 us: normalize(): center = values_in - jnp.mean(values_in, axis=-1, keepdims=True)]
  transfers between devices with their start and end apart: 9 -> 0, of which waited for: 6 -> 0; matrix products, arithmetic and copies ran while one was open for 13% -> 0% of each run, Pallas kernels for 0% -> 0%
where the time goes in v1:
time: 210 us
  Pallas kernels  189 us (90%)
  local copies, waits for them, and re-layouts  19.1 us (9%)
    pallas_call x1, Pallas kernels, fused_device(): pl.pallas_call(layer_kernel, out_shape=[jax.ShapeDtypeStruct((rows_all, w...  189 us
    unnamed x46, local copies, waits for them, and re-layouts  17.2 us

profile of v1, /device:TPU:0, one launch (start us, length us, event | category | flops | bytes accessed | tf_op | source)
XLA Modules:
  0.0 209.7 jit_solution(11542057842401558717)
XLA Ops:
  0.7 0.8 copy.36
  1.4 0.8 copy.37
  2.2 0.8 copy.38
  2.9 0.6 select_maximum_fusion.nrm_ref
  3.5 189.2 %shard_map.313 = (bf16[2048,512]{1,0:T(8,128)(2,1)}, f32[2048,512]{1,0:T(8,128)}, f32[8,128]{1,0:T(8,128)}, f32[16,1536]{1,0:T(8,128)}, f32[16,1536]{1,0:T(8,128...) custom-call(s32[8]{0:T(128)} %len_ref.1, ...), custom_call_target="tpu_custom_call" | custom-call | tf_op jit(solution)/shard_map/pallas_call | solution.py:969
  192.8 0.7 slice_bitcast_fusion
  193.5 0.7 copy.39
  194.2 0.7 copy.40
  194.8 0.7 copy.41
  195.5 1.2 slice.12
  196.7 0.0 copy-start
  196.7 3.2 %copy.56 = bf16[8,256,512]{2,1,0:T(8,128)(2,1)} copy(bf16[8,256,512]{2,1,0:T(8,128)(2,1)} %bitcast.17) | data formatting | bytes 4194304
  199.9 0.0 copy-done
  199.9 0.0 copy-start.9
  199.9 0.0 copy-start.8
  199.9 0.0 copy-start.12
  199.9 0.0 copy-start.11
  199.9 0.0 copy-start.10
  199.9 0.0 copy-start.6
  199.9 0.0 copy-start.5
  199.9 0.0 copy-start.4
  200.0 0.0 copy-start.3
  200.0 0.0 copy-start.2
  200.0 2.0 copy.57
  202.0 0.0 copy-done.9
  202.0 0.6 copy.58
  202.6 0.0 copy-done.8
  202.6 0.6 copy.59
  203.3 0.0 copy-done.7
  203.3 0.6 copy.60
  203.9 0.0 copy-done.12
  203.9 0.6 copy.61
  204.5 0.0 copy-done.11
  204.5 0.6 copy.62
  205.2 0.0 copy-done.10
  205.2 0.6 copy.63
  205.8 0.0 copy-done.6
  205.8 0.7 copy.64
  206.4 0.0 copy-done.5
  206.4 0.7 copy.65
  207.1 0.0 copy-done.4
  207.1 0.7 copy.66
  207.7 0.0 copy-done.3
  207.8 0.7 copy.67
  208.4 0.0 copy-done.2
  208.4 0.7 copy.68
  209.1 0.0 copy-done.1
  209.1 0.7 copy.69
  (2 shorter events, 0.0 us)
Async XLA Ops:
  196.7 3.2 %copy-start = (f32[2048,512]{1,0:T(8,128)S(1)}, f32[2048,512]{1,0:T(8,128)}, u32[]{:S(2)}) copy-start(f32[2048,512]{1,0:T(8,128)} %get-tuple-element.35) | copy-start | bytes 12582916
  199.9 2.1 %copy-start.9 = (f32[16,1536]{1,0:T(8,128)S(1)}, f32[16,1536]{1,0:T(8,128)}, u32[]{:S(2)}) copy-start(f32[16,1536]{1,0:T(8,128)} %get-tuple-element.92) | copy-start | bytes 294916
  199.9 2.8 %copy-start.8 = (f32[16,1536]{1,0:T(8,128)S(1)}, f32[16,1536]{1,0:T(8,128)}, u32[]{:S(2)}) copy-start(f32[16,1536]{1,0:T(8,128)} %get-tuple-element.93) | copy-start | bytes 294916
  199.9 3.4 %copy-start.7 = (f32[16,1536]{1,0:T(8,128)S(1)}, f32[16,1536]{1,0:T(8,128)}, u32[]{:S(2)}) copy-start(f32[16,1536]{1,0:T(8,128)} %get-tuple-element.94) | copy-start | bytes 294916
  199.9 4.0 %copy-start.12 = (f32[16,512]{1,0:T(8,128)S(1)}, f32[16,512]{1,0:T(8,128)}, u32[]{:S(2)}) copy-start(f32[16,512]{1,0:T(8,128)} %get-tuple-element.95) | copy-start | bytes 98308
  199.9 4.6 %copy-start.11 = (f32[16,512]{1,0:T(8,128)S(1)}, f32[16,512]{1,0:T(8,128)}, u32[]{:S(2)}) copy-start(f32[16,512]{1,0:T(8,128)} %get-tuple-element.96) | copy-start | bytes 98308
  199.9 5.2 %copy-start.10 = (f32[16,512]{1,0:T(8,128)S(1)}, f32[16,512]{1,0:T(8,128)}, u32[]{:S(2)}) copy-start(f32[16,512]{1,0:T(8,128)} %get-tuple-element.97) | copy-start | bytes 98308
  199.9 5.9 %copy-start.6 = (f32[16,2048]{1,0:T(8,128)S(1)}, f32[16,2048]{1,0:T(8,128)}, u32[]{:S(2)}) copy-start(f32[16,2048]{1,0:T(8,128)} %get-tuple-element.98) | copy-start | bytes 393220
  199.9 6.5 %copy-start.5 = (f32[16,2048]{1,0:T(8,128)S(1)}, f32[16,2048]{1,0:T(8,128)}, u32[]{:S(2)}) copy-start(f32[16,2048]{1,0:T(8,128)} %get-tuple-element.99) | copy-start | bytes 393220
  199.9 7.2 %copy-start.4 = (f32[16,2048]{1,0:T(8,128)S(1)}, f32[16,2048]{1,0:T(8,128)}, u32[]{:S(2)}) copy-start(f32[16,2048]{1,0:T(8,128)} %get-tuple-element.100) | copy-start | bytes 393220
  200.0 7.8 %copy-start.3 = (f32[64,512]{1,0:T(8,128)S(1)}, f32[64,512]{1,0:T(8,128)}, u32[]{:S(2)}) copy-start(f32[64,512]{1,0:T(8,128)} %get-tuple-element.101) | copy-start | bytes 393220
  200.0 8.4 %copy-start.2 = (f32[64,512]{1,0:T(8,128)S(1)}, f32[64,512]{1,0:T(8,128)}, u32[]{:S(2)}) copy-start(f32[64,512]{1,0:T(8,128)} %get-tuple-element.102) | copy-start | bytes 393220
  202.0 7.1 %copy-start.1 = (f32[64,512]{1,0:T(8,128)S(1)}, f32[64,512]{1,0:T(8,128)}, u32[]{:S(2)}) copy-start(f32[64,512]{1,0:T(8,128)} %get-tuple-element.103) | copy-start | bytes 393220

commit v2 on v1

--- a/solution.py
+++ b/solution.py
@@ -277,7 +277,8 @@
 NN = (((1,), (0,)), ((), ()))
 NT = (((1,), (1,)), ((), ()))
 TN = (((0,), (0,)), ((), ()))
-GATHER, REDUCE, POOL, POOLBACK, SQUARES, COPIES = 0, 24, 48, 55, 62, 72
+GATHER, SPREAD, PARTS, DOWN, OUTER, INNER, POOL, POOLBACK = 0, 22, 62, 94, 97, 105, 113, 120
+NORM_SEQ, NORM_DP, SQUARE_SEQ, SQUARE_DP, COPIES = 127, 134, 137, 144, 147
 
 
 def mm(left, right, dims=NN):
@@ -303,19 +304,16 @@
 
 def layer_kernel(
     len_ref, x_any, dy_any, wq_ref, wo_ref, wu_ref, wd_ref, nrm_ref,
-    fq_ref, fo_ref, fu_ref, fd_ref, sq_ref, so_ref, su_ref, sd_ref,
-    act_any, dx_any, gn_ref,
-    nq_ref, nfq_ref, nsq_ref, no_ref, nfo_ref, nso_ref,
-    nu_ref, nfu_ref, nsu_ref, nd_ref, nfd_ref, nsd_ref, nnrm_ref,
-    bq, bu, bd, qkv, mix, prob, gq, gu, gdt, gd,
-    r1q, r2aq, r2bq, r3aq, r3bq, r4q,
-    r1u, s2au, s2bu, r2au, r2bu, r3au, r3bu, s3u, r4u,
-    r1d, s2ad, s2bd, r2ad, r2bd, r3ad, r3bd, s3d, r4d,
-    pool_all, pool_far, pool_grad, pool_send, pool_recv, spread,
-    nrow, nacc, act_s, dup_s, h_s, ht_s, dyt_s, dh_s, fin_q, fin_u, fin_d,
-    psq, psd, x_ref, dy_ref, dx_ref, send_sem, recv_sem, local_sem,
+    act_any, dx_any, fin_q, fin_o, fin_u, fin_d, norm_sum, total_ref,
+    bkv, bqo, bu, bd, qkv, mix, prob, gq, go, yacc, h2_s, ht_s, dyt_s, act_s, dup_s,
+    own_p, s1p, r1p, s2ap, s2bp, r2ap, r2bp, r3ap, r3bp, s4p, r4p, fin_p, keep_d, s5d, r5d,
+    s2aq, s2bq, s3q, r1q, r2aq, r2bq, r3aq, r3bq, r4q,
+    s2ao, s2bo, s3o, r1o, r2ao, r2bo, r3ao, r3bo, r4o,
+    pool_all, pool_far, pool_grad, pool_send, pool_recv, live_sum, spread_w,
+    nrow, nacc, ntall, norm_seq, norm_dp, psq, psd, x_ref, dy_ref, dx_ref,
+    send_sem, recv_sem, local_sem,
 ):
-    ny, nc, nz, nx, blk, _ = bq.shape
+    ny, nc, nz, nx, blk, _ = bu.shape
     dblk = bd.shape[4]
     rows_all, width = x_ref.shape
     width3 = 3 * width
@@ -329,6 +327,8 @@
     tiles = rows_all // TILE
     per_tile = TILE // SPAN
     pairs = width // LANES
+    part_n = ff // nz
+    half_tile = TILE // 2
     dp_i = lax.axis_index("dp")
     sq_i = lax.axis_index("seq")
     y, c = dp_i // nc, dp_i % nc
@@ -340,6 +340,15 @@
     twin = dev(y, 1 - c, z, x)
     over_x = dev(y, c, z, 1 - x)
     over_y = dev(1 - y, c, z, x)
+
+    def seq_peer(step):
+        return lax.rem(sq_i + step, seq_n)
+
+    def dp_peer(step):
+        return lax.rem(dp_i + step, dp_n)
+
+    def z_peer(step):
+        return lax.rem(z + step, nz)
 
     def hop(src, dst, index, target):
         return pltpu.make_async_remote_copy(
@@ -347,29 +356,58 @@
             recv_sem=recv_sem.at[index], device_id=target, device_id_type=MESH,
         )
 
+    def start(hops):
+        for one in hops:
+            one.start()
+
+    def arrived(hops):
+        for one in hops:
+            one.wait_recv()
+
+    def sent(hops):
+        for one in hops:
+            one.wait_send()
+
+    def each(count, body):
+        def step(index, carry):
+            body(index)
+            return carry
+
+        lax.fori_loop(0, count, step, 0)
+
+    def tile_rows(tile):
+        return pl.ds(pl.multiple_of(tile * TILE, TILE), TILE)
+
     load_x = pltpu.make_async_copy(x_any, x_ref, local_sem.at[0])
     load_dy = pltpu.make_async_copy(dy_any, dy_ref, local_sem.at[1])
     keep_act = pltpu.make_async_copy(dy_ref, act_any, local_sem.at[2])
     keep_dx = pltpu.make_async_copy(dx_ref, dx_any, local_sem.at[3])
+    load_dy.start()
     load_x.start()
-    load_dy.start()
 
     barrier = pltpu.get_barrier_semaphore()
     for step in range(1, seq_n):
         pl.semaphore_signal(
-            barrier, inc=1, device_id=(dp_i, lax.rem(sq_i + step, seq_n)), device_id_type=MESH
+            barrier, inc=1, device_id=(dp_i, seq_peer(step)), device_id_type=MESH
         )
     for step in range(1, dp_n):
         pl.semaphore_signal(
-            barrier, inc=1, device_id=(lax.rem(dp_i + step, dp_n), sq_i), device_id_type=MESH
+            barrier, inc=1, device_id=(dp_peer(step), sq_i), device_id_type=MESH
         )
+
+    bkv[y, c, z, x, :, 0 : 2 * width] = wq_ref[:, width:].astype(BF)
+    bqo[y, c, z, x, :, 0:width] = wq_ref[:, 0:width].astype(BF)
+    bqo[y, c, z, x, :, width:] = wo_ref[...].astype(BF)
+    count = nrm_ref.shape[0]
+    ntall[...] = jnp.zeros_like(ntall)
+    ntall[0:count, 0:blk] = nrm_ref[...]
+    bkv[y, c, z, x, :, 2 * width :] = ntall[...].T[0:blk].astype(BF)
+    for part in range(nz):
+        for group in range(dp_n):
+            lo, at = part * part_n + group * LANES, (group * nz + part) * LANES
+            bu[y, c, z, x, :, lo : lo + LANES] = wu_ref[:, at : at + LANES].astype(BF)
+    bd[y, c, z, x] = wd_ref[...].astype(BF)
     pl.semaphore_wait(barrier, seq_n + dp_n - 2)
-
-    bq[y, c, z, x, :, 0:width3] = wq_ref[...].astype(BF)
-    bq[y, c, z, x, :, width3:] = nrm_ref[0:blk, :].astype(BF)
-    bu[y, c, z, x, :, 0:ff] = wu_ref[...].astype(BF)
-    bu[y, c, z, x, :, ff:] = wo_ref[...].astype(BF)
-    bd[y, c, z, x] = wd_ref[...].astype(BF)
 
     def gather_hops(full, base):
         cut = (full.shape[5] // 2) // LANES * LANES
@@ -379,7 +417,7 @@
             return hop(part, part, base + index, target)
 
         first = [
-            same(full.at[y, c, z, x], step - 1, dev(y, c, lax.rem(z + step, nz), x))
+            same(full.at[y, c, z, x], step - 1, dev(y, c, z_peer(step), x))
             for step in range(1, nz)
         ]
         second = [
@@ -393,61 +431,94 @@
         last = [same(full.at[:, c], 7, twin)]
         return first, second, third, last
 
-    def start(hops):
-        for one in hops:
-            one.start()
-
-    def arrived(hops):
-        for one in hops:
-            one.wait_recv()
-
-    def sent(hops):
-        for one in hops:
-            one.wait_send()
-
-    hops_q = gather_hops(bq, GATHER)
-    hops_u = gather_hops(bu, GATHER + 8)
-    hops_d = gather_hops(bd, GATHER + 16)
-    start(hops_q[0])
-    start(hops_u[0])
-    start(hops_d[0])
-
-    def clear(index, carry):
-        gq[...] = jnp.zeros_like(gq)
-        gu[...] = jnp.zeros_like(gu)
-        gdt[...] = jnp.zeros_like(gdt)
-        return carry
-
-    lax.fori_loop(0, 1, clear, 0)
+    def direct(full, base):
+        mine = full.at[y, c, z, x]
+        return [
+            hop(mine, mine, base + step - 1, dev(y, c, z_peer(step), x)) for step in range(1, nz)
+        ]
+
+    def spread_hops(part):
+        base = SPREAD + part * 10
+        cols = pl.ds(pl.multiple_of(part * part_n, part_n), part_n)
+        one = pl.ds(pl.multiple_of(part * part_n, LANES), part_n // 2)
+        two = pl.ds(pl.multiple_of(part * part_n + part_n // 2, LANES), part_n // 2)
+        d_one, d_two = pl.ds(0, width // 2), pl.ds(width // 2, width // 2)
+
+        def same(place, index, target):
+            return hop(place, place, base + index, target)
+
+        return (
+            [
+                same(bu.at[y, c, :, x, :, one], 0, over_x),
+                same(bu.at[y, c, :, x, :, two], 1, over_y),
+                same(bd.at[y, c, part, x, :, d_one], 2, over_x),
+                same(bd.at[y, c, part, x, :, d_two], 3, over_y),
+            ],
+            [
+                same(bu.at[y, c, :, :, :, one], 4, over_y),
+                same(bu.at[:, c, :, x, :, two], 5, over_x),
+                same(bd.at[y, c, part, :, :, d_one], 6, over_y),
+                same(bd.at[:, c, part, x, :, d_two], 7, over_x),
+            ],
+            [
+                same(bu.at[:, c, :, :, :, cols], 8, twin),
+                same(bd.at[:, c, part], 9, twin),
+            ],
+        )
+
+    def pass_on(part, stage):
+        hops = spread_hops(part)
+        arrived(hops[stage])
+        start(hops[stage + 1])
+
+    hops_kv = gather_hops(bkv, GATHER)
+    hops_qo = gather_hops(bqo, GATHER + 8)
+    direct_u = direct(bu, GATHER + 16)
+    direct_d = direct(bd, GATHER + 19)
+    start(hops_kv[0])
+    start(hops_qo[0])
+    start(direct_u)
+    start(direct_d)
     nacc[...] = jnp.zeros_like(nacc)
     pool_grad[...] = jnp.zeros_like(pool_grad)
-
+    arrived(hops_kv[0])
+    start(hops_kv[1])
+    load_dy.wait()
+
+    def turn_dy(tile):
+        rows = tile_rows(tile)
+        dyt_s[:, rows] = dy_ref[rows, :].astype(F32).T.astype(BF)
+
+    each(tiles // 2, turn_dy)
+    arrived(hops_kv[1])
+    start(hops_kv[2])
+    arrived(hops_qo[0])
+    start(hops_qo[1])
     load_x.wait()
-    arrived(hops_q[0])
-    start(hops_q[1])
-    arrived(hops_q[1])
-    start(hops_q[2])
-    arrived(hops_q[2])
-    start(hops_q[3])
-    arrived(hops_u[0])
-    start(hops_u[1])
-    arrived(hops_d[0])
-    start(hops_d[1])
-    arrived(hops_q[3])
-
-    norm_cols = bq[:, :, :, :, :, width3:].reshape(width, LANES).astype(F32)
+    each(tiles // 2, lambda tile: turn_dy(tile + tiles // 2))
+    arrived(hops_kv[2])
+    start(hops_kv[3])
+    arrived(hops_qo[1])
+    start(hops_qo[2])
+    arrived(direct_u)
+    arrived(direct_d)
+    for part in range(nz):
+        start(spread_hops(part)[0])
+    arrived(hops_kv[3])
+
+    norm_cols = bkv[:, :, :, :, :, 2 * width :].reshape(width, LANES).astype(F32)
     nrow[...] = norm_cols.T[0:8]
 
-    def w_qkv(lo, hi):
-        return bq[:, :, :, :, :, lo:hi].reshape(width, hi - lo)
-
-    def qkv_tile(tile, pooled):
-        rows = pl.ds(pl.multiple_of(tile * TILE, TILE), TILE)
-        hat, _ = centered(x_ref[rows, :].astype(F32))
-        h1 = (hat * nrow[0:1, :] + nrow[1:2, :]).astype(BF)
-        for part in range(3):
-            cols = pl.ds(part * width, width)
-            qkv[rows, cols] = mm(h1, w_qkv(part * width, (part + 1) * width)).astype(BF)
+    def w_qkv(part):
+        if part == 0:
+            return bqo[:, :, :, :, :, 0:width].reshape(width, width)
+        return bkv[:, :, :, :, :, (part - 1) * width : part * width].reshape(width, width)
+
+    def first_norm(rows):
+        hat, scale = centered(x_ref[rows, :].astype(F32))
+        return hat, scale, (hat * nrow[0:1, :] + nrow[1:2, :]).astype(BF)
+
+    def live_pick(tile):
         block_at = lax.broadcasted_iota(jnp.int32, (blocks, TILE), 0)
         row_at = lax.broadcasted_iota(jnp.int32, (blocks, TILE), 1) + tile * TILE
         pos = sq_i * local_len + lax.rem(row_at, local_len)
@@ -456,21 +527,23 @@
         for i in range(TILE // local_len):
             at = tile * (TILE // local_len) + i
             length = jnp.where(item == at, len_ref[at], length)
-        pick = jnp.where((row_at // SPAN == block_at) & (pos < length), 1.0, 0.0).astype(BF)
-
-        @pl.when(tile == 1)
+        return jnp.where((row_at // SPAN == block_at) & (pos < length), 1.0, 0.0).astype(BF)
+
+    def kv_tile(tile, pooled):
+        rows = tile_rows(tile)
+        _, _, h1 = first_norm(rows)
+        h2_s[rows, :] = h1
+        for part in (1, 2):
+            qkv[rows, pl.ds(part * width, width)] = mm(h1, w_qkv(part)).astype(BF)
+
+        @pl.when(tile == 3)
         def _():
-            arrived(hops_u[1])
-            start(hops_u[2])
-
-        @pl.when(tile == 2)
-        def _():
-            arrived(hops_d[1])
-            start(hops_d[2])
-
-        return pooled + mm(pick, qkv[rows, width:])
-
-    pooled = lax.fori_loop(0, tiles, qkv_tile, jnp.zeros((blocks, 2 * width), F32))
+            arrived(hops_qo[2])
+            start(hops_qo[3])
+
+        return pooled + mm(live_pick(tile), qkv[rows, width:])
+
+    pooled = lax.fori_loop(0, tiles, kv_tile, jnp.zeros((blocks, 2 * width), F32))
     block_col = lax.broadcasted_iota(jnp.int32, (blocks, 1), 0)
     length_col = jnp.zeros((blocks, 1), jnp.int32)
     for i in range(blocks // spans_here):
@@ -479,17 +552,18 @@
     count_col = jnp.clip(length_col - first_pos, 1, SPAN).astype(F32)
     pool_all[sq_i] = (pooled / count_col).astype(BF)
     pool_hops = [
-        hop(
-            pool_all.at[sq_i], pool_all.at[sq_i], POOL + step - 1,
-            (dp_i, lax.rem(sq_i + step, seq_n)),
-        )
+        hop(pool_all.at[sq_i], pool_all.at[sq_i], POOL + step - 1, (dp_i, seq_peer(step)))
         for step in range(1, seq_n)
     ]
     start(pool_hops)
-    arrived(hops_u[2])
-    start(hops_u[3])
-    arrived(hops_d[2])
-    start(hops_d[3])
+    pass_on(0, 0)
+    arrived(hops_qo[3])
+
+    def q_tile(tile):
+        rows = tile_rows(tile)
+        qkv[rows, 0:width] = mm(h2_s[rows, :], w_qkv(0)).astype(BF)
+
+    each(tiles, q_tile)
     arrived(pool_hops)
 
     far_n = seq_n * blocks
@@ -509,10 +583,8 @@
     grad_a, grad_b = half_a.astype(BF), half_b.astype(BF)
 
     def both(near_rows, far_rows, cols):
-        return jnp.concatenate([qkv[near_rows, cols], pool_far[far_rows, cols_far(cols)]], axis=0)
-
-    def cols_far(cols):
-        return pl.ds(cols.start - width, cols.size)
+        far_cols = pl.ds(cols.start - width, cols.size)
+        return jnp.concatenate([qkv[near_rows, cols], pool_far[far_rows, far_cols]], axis=0)
 
     def diagonal(stacked):
         return jnp.concatenate(
@@ -520,6 +592,14 @@
         ).T
 
     def attend(block, carry):
+        for at, part, stage in (
+            (0, 1, 0), (3, 0, 1), (4, 2, 0), (7, 1, 1), (8, 3, 0), (12, 2, 1), (15, 3, 1)
+        ):
+
+            @pl.when(block == at)
+            def _(part=part, stage=stage):
+                pass_on(part, stage)
+
         item = block // spans_here
         sub = lax.rem(block, spans_here)
         rows = pl.ds(pl.multiple_of(block * SPAN, SPAN), SPAN)
@@ -546,40 +626,137 @@
         return carry
 
     lax.fori_loop(0, blocks, attend, 0)
-    arrived(hops_u[3])
-    arrived(hops_d[3])
-    for hops in (hops_q, hops_u, hops_d):
-        for group in hops:
-            sent(group)
-    sent(pool_hops)
-
-    load_dy.wait()
-    w_out = bu[:, :, :, :, :, ff:].reshape(width, width)
+    for group in (*hops_kv, *hops_qo, direct_u, direct_d, pool_hops):
+        sent(group)
+
+    w_out = bqo[:, :, :, :, :, width:].reshape(width, width)
     gelu_in = math.sqrt(2.0 / math.pi)
     gelu_cube = 0.044715
 
-    tall_tile = (nz, nx, dblk, width)
-    half_tile = TILE // 2
-
-    def ffn_tile(tile, carry):
-        rows = pl.ds(pl.multiple_of(tile * TILE, TILE), TILE)
+    def second_norm(rows):
         x1 = x_ref[rows, :].astype(F32) + mm(mix[rows, :], w_out)
         hat, scale = centered(x1)
-        gd[0] = x1.reshape(tall_tile)
-        gd[1] = hat.reshape(tall_tile)
+        return x1, hat, scale
+
+    def ffn_open(tile):
+        rows = tile_rows(tile)
+        x1, hat, _ = second_norm(rows)
+        yacc[rows, :] = x1
+        dx_ref[rows, :] = jnp.zeros((TILE, width), F32)
         h2 = hat * nrow[2:3, :] + nrow[3:4, :]
-        h_s[...] = h2.astype(BF)
-        ht_s[...] = h2.T.astype(BF)
-        dyt_s[...] = dy_ref[rows, :].astype(F32).T.astype(BF)
-        dh_s[...] = jnp.zeros_like(dh_s)
-
-        def ffn_part(part, inner):
-            cols = pl.ds(pl.multiple_of(part * TILE, TILE), TILE)
-            w_up = bu[:, :, :, :, :, cols].reshape(width, TILE)
-            w_down = bd[part // nc, part % nc].reshape(TILE, width)
-            for part_rows in range(2):
-                some = pl.ds(part_rows * half_tile, half_tile)
-                up = mm(h_s[some, :], w_up)
+        h2_s[rows, :] = h2.astype(BF)
+        ht_s[:, rows] = h2.T.astype(BF)
+
+    each(tiles, ffn_open)
+
+    half_cols = width // 2
+    one_p, two_p = pl.ds(0, half_cols), pl.ds(half_cols, half_cols)
+    up_rows = nz * blk
+
+    def part_hops(part):
+        base = PARTS + part * 8
+        return (
+            [hop(s1p, r1p.at[part], base, twin)],
+            [
+                hop(s1p.at[1 - y, :, :, one_p], r2ap.at[part], base + 1, over_y),
+                hop(s1p.at[:, 1 - x, :, two_p], r2bp.at[part], base + 2, over_x),
+            ],
+            [
+                hop(s2ap.at[1 - x], r3ap.at[part], base + 3, over_x),
+                hop(s2bp.at[1 - y], r3bp.at[part], base + 4, over_y),
+            ],
+            [
+                hop(
+                    s4p.at[part, z_peer(step)], r4p.at[step - 1, part], base + 4 + step,
+                    dev(y, c, z_peer(step), x),
+                )
+                for step in range(1, nz)
+            ],
+        )
+
+    def down_cols(group):
+        cols = pl.ds(pl.multiple_of(group * LANES, LANES), LANES)
+        return gq[:, :, :, :, :, cols].reshape(width, LANES)
+
+    def part_first(part):
+        for yy in range(ny):
+            for xx in range(nx):
+                for zz in range(nz):
+                    at = pl.ds(zz * blk, blk)
+                    own_p[yy, xx, at] = go[yy, c, zz, xx]
+                    s1p[yy, xx, at] = go[yy, 1 - c, zz, xx].astype(BF)
+            mine = down_cols(yy * nc + c).T
+            other = down_cols(yy * nc + 1 - c).T
+            for xx in range(nx):
+                own_p[yy, xx, up_rows:] = mine[xx * dblk : (xx + 1) * dblk]
+                s1p[yy, xx, up_rows:] = other[xx * dblk : (xx + 1) * dblk].astype(BF)
+        start(part_hops(part)[0])
+
+    def part_second(part):
+        hops = part_hops(part)
+        arrived(hops[0])
+        sent(hops[0])
+
+        def add(index):
+            yy, xx = index // nx, index % nx
+            total = own_p[yy, xx] + r1p[part, yy, xx].astype(F32)
+            own_p[yy, xx] = total
+            s1p[yy, xx] = total.astype(BF)
+
+        each(ny * nx, add)
+        start(hops[1])
+
+    def part_third(part):
+        hops = part_hops(part)
+        arrived(hops[1])
+        sent(hops[1])
+        for xx in range(nx):
+            total = own_p[y, xx, :, one_p] + r2ap[part, xx].astype(F32)
+            own_p[y, xx, :, one_p] = total
+            s2ap[xx] = total.astype(BF)
+        for yy in range(ny):
+            total = own_p[yy, x, :, two_p] + r2bp[part, yy].astype(F32)
+            own_p[yy, x, :, two_p] = total
+            s2bp[yy] = total.astype(BF)
+        start(hops[2])
+
+    def part_fourth(part):
+        hops = part_hops(part)
+        arrived(hops[2])
+        sent(hops[2])
+        own_p[y, x, :, one_p] += r3ap[part].astype(F32)
+        own_p[y, x, :, two_p] += r3bp[part].astype(F32)
+        for zz in range(nz):
+            s4p[part, zz] = own_p[y, x, zz * blk : (zz + 1) * blk].astype(BF)
+        fin_p[part] = own_p[y, x, pl.ds(pl.multiple_of(z * blk, blk), blk)]
+        down = own_p[y, x, up_rows:]
+        keep_d[part] = down
+        s5d[part] = down.astype(BF)
+        start(hops[3])
+
+    down_hops = [
+        hop(
+            s5d.at[z_peer(step)], r5d.at[step - 1], DOWN + step - 1, dev(y, c, z_peer(step), x)
+        )
+        for step in range(1, nz)
+    ]
+
+    def ffn_part(part, carry):
+        cols = pl.ds(pl.multiple_of(part * part_n, part_n), part_n)
+        arrived(spread_hops(part)[2])
+        w_up = bu[:, :, :, :, :, cols].reshape(width, part_n)
+        w_down = bd[:, :, part].reshape(part_n, width)
+
+        def ffn_tile(tile):
+            @pl.when((part > 0) & (tile == 1))
+            def _():
+                part_second(part - 1)
+
+            rows = tile_rows(tile)
+            for piece in range(2):
+                lo = tile * TILE + piece * half_tile
+                some = pl.ds(pl.multiple_of(lo, half_tile), half_tile)
+                up = mm(h2_s[some, :], w_up)
                 square = up * up
                 bent = jnp.tanh(up * (gelu_in + (gelu_in * gelu_cube) * square))
                 half = 0.5 + 0.5 * bent
@@ -587,40 +764,55 @@
                 rate = half + (up * (1.0 - bent * bent)) * (
                     0.5 * gelu_in + (1.5 * gelu_in * gelu_cube) * square
                 )
-                near = pl.ds(pl.multiple_of(tile * TILE + part_rows * half_tile, half_tile), half_tile)
-                dup_s[some, :] = (mm(dy_ref[near, :], w_down, NT) * rate).astype(BF)
-            gd[0] += mm(act_s[...], w_down).reshape(tall_tile)
-            gdt[:, cols] += mm(dyt_s[...], act_s[...])
-            gu[:, :, :, :, :, cols] += mm(ht_s[...], dup_s[...]).reshape(
-                ny, nc, nz, nx, blk, TILE
-            )
-            dh_s[...] += mm(dup_s[...], w_up, NT)
-            return inner
-
-        lax.fori_loop(0, ff // TILE, ffn_part, 0)
-        dh2 = dh_s[...]
-        hat = gd[1].reshape(TILE, width)
+                dup_s[some, :] = (mm(dy_ref[some, :], w_down, NT) * rate).astype(BF)
+            yacc[rows, :] += mm(act_s[rows, :], w_down)
+            dx_ref[rows, :] += mm(dup_s[rows, :], w_up, NT)
+
+        each(tiles, ffn_tile)
+
+        @pl.when(part > 0)
+        def _():
+            part_third(part - 1)
+
+        gq[:, :, :, :, :, 0:part_n] = mm(dyt_s[...], act_s[...]).reshape(go.shape)
+        go[...] = mm(ht_s[...], dup_s[...]).reshape(go.shape)
+
+        @pl.when(part > 0)
+        def _():
+            part_fourth(part - 1)
+
+        part_first(part)
+        return carry
+
+    lax.fori_loop(0, nz, ffn_part, 0)
+
+    def ffn_close(tile):
+        @pl.when(tile == 1)
+        def _():
+            part_second(nz - 1)
+
+        rows = tile_rows(tile)
+        _, hat, scale = second_norm(rows)
+        dh2 = dx_ref[rows, :]
         nacc[2] += fold_rows(dh2 * hat)
         nacc[3] += fold_rows(dh2)
         dx1 = dy_ref[rows, :].astype(F32) + norm_back(dh2 * nrow[2:3, :], hat, scale)
-        dy_ref[rows, :] = gd[0].reshape(TILE, width).astype(BF)
+        dy_ref[rows, :] = yacc[rows, :].astype(BF)
         dx_ref[rows, :] = dx1
         dz = dx1.astype(BF)
-        gu[:, :, :, :, :, ff:] += mm(mix[rows, :], dz, TN).reshape(ny, nc, nz, nx, blk, width)
+        act_s[rows, :] = dz
+        ht_s[:, rows] = mix[rows, :].astype(F32).T.astype(BF)
         mix[rows, :] = mm(dz, w_out, NT).astype(BF)
-        return carry
-
-    lax.fori_loop(0, tiles, ffn_tile, 0)
+
+    each(tiles, ffn_close)
     keep_act.start()
-
-    def each(count, body):
-        def step(index, carry):
-            body(index)
-            return carry
-
-        lax.fori_loop(0, count, step, 0)
-
-    def reduce_steps(own, load_other, s1, r1, s2a, s2b, r2a, r2b, r3a, r3b, s3, r4, fin, base):
+    for part in range(nz):
+        for group in spread_hops(part):
+            sent(group)
+    go[...] = mm(ht_s[...], act_s[...]).reshape(go.shape)
+
+    def reduce_steps(full, s1, r1, s2a, s2b, r2a, r2b, r3a, r3b, s3, r4, fin, base):
+        own = full.at[:, c]
         n = s1.shape[4]
         cut = (n // 2) // LANES * LANES
         one, two = pl.ds(0, cut), pl.ds(cut, n - cut)
@@ -635,14 +827,21 @@
         ]
         hop4 = [
             hop(
-                s3.at[lax.rem(z + step, nz)], r4.at[step - 1], base + 4 + step,
-                dev(y, c, lax.rem(z + step, nz), x),
+                s3.at[z_peer(step)], r4.at[step - 1], base + 4 + step,
+                dev(y, c, z_peer(step), x),
             )
             for step in range(1, nz)
         ]
 
+        def places(index):
+            return index // (nz * nx), (index // nx) % nz, index % nx
+
         def stage1():
-            load_other()
+            def load(index):
+                yy, zz, xx = places(index)
+                s1[yy, zz, xx] = full[yy, 1 - c, zz, xx].astype(BF)
+
+            each(ny * nz * nx, load)
             start(hop1)
 
         def stage2():
@@ -650,7 +849,7 @@
             sent(hop1)
 
             def add(index):
-                yy, zz, xx = index // (nz * nx), (index // nx) % nz, index % nx
+                yy, zz, xx = places(index)
                 total = own[yy, zz, xx] + r1[yy, zz, xx].astype(F32)
                 own[yy, zz, xx] = total
                 s1[yy, zz, xx] = total.astype(BF)
@@ -665,13 +864,13 @@
                     total = own[y, zz, xx, :, one] + r2a[zz, xx].astype(F32)
                     own[y, zz, xx, :, one] = total
                     s2a[zz, xx] = total.astype(BF)
-            hop3[0].start()
+            start(hop3[0:1])
             for yy in range(ny):
                 for zz in range(nz):
                     total = own[yy, zz, x, :, two] + r2b[yy, zz].astype(F32)
                     own[yy, zz, x, :, two] = total
                     s2b[yy, zz] = total.astype(BF)
-            hop3[1].start()
+            start(hop3[1:2])
 
         def stage4():
             arrived(hop3)
@@ -696,61 +895,31 @@
 
         return stage1, stage2, stage3, stage4, stage5
 
-    def plain_own(full):
-        return full.at[:, c]
-
-    def plain_other(full, s1):
-        def load():
-            def one(index):
-                yy, zz, xx = index // (nz * nx), (index // nx) % nz, index % nx
-                s1[yy, zz, xx] = full[yy, 1 - c, zz, xx].astype(BF)
-
-            each(ny * nz * nx, one)
-
-        return load
-
-    def down_other():
-        group = nz * nx * dblk
-        for yy in range(ny):
-            for cc, is_own in ((c, True), (1 - c, False)):
-                for part in range(group // LANES):
-                    at = pl.multiple_of((yy * nc + cc) * group + part * LANES, LANES)
-                    piece = gdt[:, pl.ds(at, LANES)].T.reshape(LANES // dblk, dblk, width)
-                    for inner in range(LANES // dblk):
-                        where = part * (LANES // dblk) + inner
-                        if is_own:
-                            gd[yy, where // nx, where % nx] = piece[inner]
-                        else:
-                            s1d[yy, where // nx, where % nx] = piece[inner].astype(BF)
-
-    s1u, s1d = bu.at[:, 0], bd.at[:, 0]
-    cols_q = r1q.shape[4]
-    cut_q = r3aq.shape[2]
-    s1q = bu.at[:, 1, :, :, :, pl.ds(0, cols_q)]
-    s2aq = s2au.at[:, :, :, pl.ds(0, cut_q)]
-    s2bq = s2bu.at[:, :, :, pl.ds(0, cols_q - cut_q)]
-    s3q = s3u.at[:, :, pl.ds(0, cols_q)]
-    red_d = reduce_steps(
-        gd, down_other, s1d, r1d, s2ad, s2bd, r2ad, r2bd, r3ad, r3bd, s3d, r4d, fin_d, REDUCE
-    )
-    red_u = reduce_steps(
-        plain_own(gu), plain_other(gu, s1u), s1u, r1u, s2au, s2bu, r2au, r2bu, r3au, r3bu,
-        s3u, r4u, fin_u, REDUCE + 8,
+    red_o = reduce_steps(
+        go, bu.at[:, 0, :, :, :, pl.ds(0, width)], r1o, s2ao, s2bo, r2ao, r2bo, r3ao, r3bo, s3o,
+        r4o, fin_o, OUTER,
     )
     red_q = reduce_steps(
-        plain_own(gq), plain_other(gq, s1q), s1q, r1q, s2aq, s2bq, r2aq, r2bq, r3aq, r3bq,
-        s3q, r4q, fin_q, REDUCE + 16,
-    )
-    red_d[0]()
-    red_u[0]()
+        gq, bu.at[:, 1, :, :, :, pl.ds(0, width3)], r1q, s2aq, s2bq, r2aq, r2bq, r3aq, r3bq,
+        s3q, r4q, fin_q, INNER,
+    )
+    red_o[0]()
+
+    def last_third():
+        part_third(nz - 1)
+
+    def fourth_and_down():
+        part_fourth(nz - 1)
+        start(down_hops)
 
     def attend_back(block, carry):
-        for at, steps in ((1, 1), (5, 2), (10, 3)):
+        for at, step in (
+            (0, last_third), (5, fourth_and_down), (6, red_o[1]), (10, red_o[2]), (14, red_o[3])
+        ):
 
             @pl.when(block == at)
-            def _(steps=steps):
-                red_d[steps]()
-                red_u[steps]()
+            def _(step=step):
+                step()
 
         item = block // spans_here
         rows = pl.ds(pl.multiple_of(block * SPAN, SPAN), SPAN)
@@ -792,89 +961,144 @@
     )
     back_hops = [
         hop(
-            pool_send.at[lax.rem(sq_i + step, seq_n)], pool_recv.at[step - 1],
-            POOLBACK + step - 1, (dp_i, lax.rem(sq_i + step, seq_n)),
+            pool_send.at[seq_peer(step)], pool_recv.at[step - 1], POOLBACK + step - 1,
+            (dp_i, seq_peer(step)),
         )
         for step in range(1, seq_n)
     ]
     start(back_hops)
+
+    live_sum[...] = jnp.zeros_like(live_sum)
+
+    def turn_h1(tile):
+        rows = tile_rows(tile)
+        _, _, h1 = first_norm(rows)
+        ht_s[:, rows] = h1.astype(F32).T.astype(BF)
+        live_sum[...] += mm(live_pick(tile), h1)
+
+    each(tiles, turn_h1)
+    for part in range(3):
+        cols = pl.ds(part * width, width)
+        gq[:, :, :, :, :, cols] = mm(ht_s[...], qkv[:, cols]).reshape(
+            ny, nc, nz, nx, blk, width
+        )
+    for part in range(nz):
+        arrived(part_hops(part)[3])
+        total = fin_p[part]
+        for step in range(nz - 1):
+            total = total + r4p[step, part].astype(F32)
+        for group in range(dp_n):
+            at = (group * nz + part) * LANES
+            fin_u[:, at : at + LANES] = total[:, group * LANES : (group + 1) * LANES]
+    arrived(down_hops)
+    total = keep_d[z]
+    for step in range(nz - 1):
+        total = total + r5d[step].astype(F32)
+    fin_d[...] = total
+    red_o[4]()
+
     arrived(back_hops)
     pool_total = pool_send[sq_i].astype(F32)
     for step in range(seq_n - 1):
         pool_total = pool_total + pool_recv[step].astype(F32)
-    spread[...] = pool_total / count_col
-
-    def last_tile(tile, carry):
-        rows = pl.ds(pl.multiple_of(tile * TILE, TILE), TILE)
-        hat, scale = centered(x_ref[rows, :].astype(F32))
-        h1 = (hat * nrow[0:1, :] + nrow[1:2, :]).astype(BF)
+    far = pool_total / count_col
+    far_hi = far.astype(BF)
+    far_lo = (far - far_hi.astype(F32)).astype(BF)
+    near = live_sum[...]
+    near_hi = near.astype(BF)
+    near_lo = (near - near_hi.astype(F32)).astype(BF)
+    left = jnp.concatenate([near_hi, near_lo, near_hi], axis=0)
+    right = jnp.concatenate([far_hi, far_hi, far_lo], axis=0)
+    for part in range(2):
+        cols = pl.ds((part + 1) * width, width)
+        gq[:, :, :, :, :, cols] += mm(left, right[:, part * width : (part + 1) * width], TN).reshape(
+            ny, nc, nz, nx, blk, width
+        )
+    red_q[0]()
+    far_two = jnp.concatenate([far_hi, far_lo], axis=0)
+    both_far = mm(far_two[:, 0:width], w_qkv(1), NT) + mm(far_two[:, width:], w_qkv(2), NT)
+    spread_w[...] = both_far[0:blocks] + both_far[blocks:]
+
+    def last_tile(tile):
+        for at, step in ((1, red_q[1]), (3, red_q[2])):
+
+            @pl.when(tile == at)
+            def _(step=step):
+                step()
+
+        rows = tile_rows(tile)
+        hat, scale, _ = first_norm(rows)
+        extra = []
         for part in range(per_tile):
             block = tile * per_tile + part
-            own_rows = pl.ds(pl.multiple_of(block * SPAN, SPAN), SPAN)
             pos = (
                 sq_i * local_len
                 + lax.rem(block, spans_here) * SPAN
                 + lax.broadcasted_iota(jnp.int32, (SPAN, 1), 0)
             )
             live = jnp.where(pos < len_ref[block // spans_here], 1.0, 0.0)
-            far = live * spread[pl.ds(block, 1), :]
-            qkv[own_rows, width:] = (qkv[own_rows, width:].astype(F32) + far).astype(BF)
-        ht_s[...] = h1.astype(F32).T.astype(BF)
-        dh_s[...] = jnp.zeros_like(dh_s)
+            extra.append(live * spread_w[pl.ds(block, 1), :])
+        dh1 = jnp.concatenate(extra, axis=0)
         for part in range(3):
-            cols = pl.ds(part * width, width)
-            gq[:, :, :, :, :, cols] += mm(ht_s[...], qkv[rows, cols]).reshape(
-                ny, nc, nz, nx, blk, width
-            )
-            dh_s[...] += mm(qkv[rows, cols], w_qkv(part * width, (part + 1) * width), NT)
-        dh1 = dh_s[...]
+            dh1 = dh1 + mm(qkv[rows, pl.ds(part * width, width)], w_qkv(part), NT)
         nacc[0] += fold_rows(dh1 * hat)
         nacc[1] += fold_rows(dh1)
         dx_ref[rows, :] += norm_back(dh1 * nrow[0:1, :], hat, scale)
-        return carry
-
-    lax.fori_loop(0, tiles, last_tile, 0)
+
+    each(tiles, last_tile)
     keep_dx.start()
     norm_rows = [jnp.sum(nacc[k], axis=0, keepdims=True) for k in range(4)]
-    norm_rows.append(jnp.zeros((LANES - 4, width), F32))
-    gq[:, :, :, :, :, width3:] = (
-        jnp.concatenate(norm_rows, axis=0).T.reshape(ny, nc, nz, nx, blk, LANES)
-    )
-    red_q[0]()
-    red_d[4]()
-    red_u[4]()
-    red_q[1]()
-    red_q[2]()
+    norm_rows.append(jnp.zeros((4, width), F32))
+    norm_seq[sq_i] = jnp.concatenate(norm_rows, axis=0)
+    norm_hops = [
+        hop(norm_seq.at[sq_i], norm_seq.at[sq_i], NORM_SEQ + step - 1, (dp_i, seq_peer(step)))
+        for step in range(1, seq_n)
+    ]
+    norm_hops_dp = [
+        hop(norm_dp.at[dp_i], norm_dp.at[dp_i], NORM_DP + step - 1, (dp_peer(step), sq_i))
+        for step in range(1, dp_n)
+    ]
+    start(norm_hops)
     red_q[3]()
-    sent(back_hops)
-    red_q[4]()
-
-    def partial(ref):
-        values_in = ref[...]
+    arrived(norm_hops)
+    total = norm_seq[0]
+    for k in range(1, seq_n):
+        total = total + norm_seq[k]
+    norm_dp[dp_i] = total
+    start(norm_hops_dp)
+
+    def partial(values_in):
         squares = fold_rows(values_in * values_in)
         return sum(
             squares[:, k * LANES : (k + 1) * LANES] for k in range(squares.shape[1] // LANES)
         )
 
-    psq[sq_i] = partial(fin_q) + partial(fin_u) + partial(fin_d)
+    early = partial(fin_u[...]) + partial(fin_d[...]) + partial(fin_o[...])
+    red_q[4]()
+    psq[sq_i] = early + partial(fin_q[...])
     seq_hops = [
-        hop(
-            psq.at[sq_i], psq.at[sq_i], SQUARES + step - 1,
-            (dp_i, lax.rem(sq_i + step, seq_n)),
-        )
+        hop(psq.at[sq_i], psq.at[sq_i], SQUARE_SEQ + step - 1, (dp_i, seq_peer(step)))
         for step in range(1, seq_n)
     ]
     start(seq_hops)
+    sent(back_hops)
+    for part in range(nz):
+        sent(part_hops(part)[3])
+    sent(down_hops)
+    sent(norm_hops)
+    arrived(norm_hops_dp)
+    sent(norm_hops_dp)
+    total = norm_dp[0]
+    for k in range(1, dp_n):
+        total = total + norm_dp[k]
+    norm_sum[...] = total
     arrived(seq_hops)
     total = psq[0]
     for k in range(1, seq_n):
         total = total + psq[k]
     psd[dp_i] = total
     dp_hops = [
-        hop(
-            psd.at[dp_i], psd.at[dp_i], SQUARES + seq_n - 2 + step,
-            (lax.rem(dp_i + step, dp_n), sq_i),
-        )
+        hop(psd.at[dp_i], psd.at[dp_i], SQUARE_DP + step - 1, (dp_peer(step), sq_i))
         for step in range(1, dp_n)
     ]
     start(dp_hops)
@@ -882,45 +1106,66 @@
     total = psd[0]
     for k in range(1, dp_n):
         total = total + psd[k]
-    grad_norm = jnp.sqrt(jnp.sum(jnp.sum(total, axis=1, keepdims=True), axis=0, keepdims=True))
+    total_ref[...] = total
+    sent(seq_hops)
+    sent(dp_hops)
+    keep_act.wait()
+    keep_dx.wait()
+
+
+def update_kernel(
+    act_in, dx_in, total_ref, gq_ref, go_ref, gu_ref, gd_ref, gn_ref,
+    wq_ref, wo_ref, wu_ref, wd_ref, wn_ref, fq_ref, fo_ref, fu_ref, fd_ref, fn_ref,
+    sq_ref, so_ref, su_ref, sd_ref, sn_ref,
+    act_out, dx_out, norm_ref, nq, nfq, nsq, no, nfo, nso, nu, nfu, nsu, nd, nfd, nsd,
+    nn, nfn, nsn, act_s, dx_s, sems_in, sems_out,
+):
+    pieces = 4
+    piece = act_s.shape[0] // pieces
+    moves = []
+    for k in range(pieces):
+        rows = pl.ds(k * piece, piece)
+        for n, (src, mid, dst) in enumerate(
+            ((dx_in, dx_s, dx_out), (act_in, act_s, act_out))
+        ):
+            moves.append((
+                pltpu.make_async_copy(src.at[rows], mid.at[rows], sems_in.at[n * pieces + k]),
+                pltpu.make_async_copy(mid.at[rows], dst.at[rows], sems_out.at[n * pieces + k]),
+            ))
+    for inward, _ in moves:
+        inward.start()
+    norm_grads = gn_ref[...]
+    total = jnp.sum(total_ref[...]) + jnp.sum(norm_grads * norm_grads)
+    total = jnp.full((1, 1), total, F32)
+    grad_norm = jnp.sqrt(total)
     factor = clip_bound / jnp.maximum(grad_norm, clip_bound)
-    gn_ref[...] = jnp.broadcast_to(grad_norm, gn_ref.shape)
+    norm_ref[...] = grad_norm
 
     def update(weight, grad_in, first, second, outs, rate, decay):
         new = adamw_update(weight, grad_in, first, second, factor, rate, decay)
         for out, value in zip(outs, new):
             out[...] = value
 
+    for inward, outward in moves:
+        inward.wait()
+        outward.start()
+    for w, g, m, s, outs in (
+        (wq_ref, gq_ref, fq_ref, sq_ref, (nq, nfq, nsq)),
+        (wo_ref, go_ref, fo_ref, so_ref, (no, nfo, nso)),
+        (wu_ref, gu_ref, fu_ref, su_ref, (nu, nfu, nsu)),
+        (wd_ref, gd_ref, fd_ref, sd_ref, (nd, nfd, nsd)),
+    ):
+        update(w[...], g[...], m[...], s[...], outs, rate_matrix, decay_coef)
+    count, cols = wn_ref.shape
+    width = norm_grads.shape[1]
+    place = (lax.axis_index("dp") * lax.axis_size("seq") + lax.axis_index("seq")) * cols
+    turned = pltpu.roll(norm_grads, lax.rem(width - place, width), 1)
     update(
-        wq_ref[...], fin_q[:, 0:width3], fq_ref[...], sq_ref[...],
-        (nq_ref, nfq_ref, nsq_ref), rate_matrix, decay_coef,
-    )
-    update(
-        wo_ref[...], fin_u[:, ff:], fo_ref[...], so_ref[...],
-        (no_ref, nfo_ref, nso_ref), rate_matrix, decay_coef,
-    )
-    update(
-        wu_ref[...], fin_u[:, 0:ff], fu_ref[...], su_ref[...],
-        (nu_ref, nfu_ref, nsu_ref), rate_matrix, decay_coef,
-    )
-    update(
-        wd_ref[...], fin_d[...], fd_ref[...], sd_ref[...],
-        (nd_ref, nfd_ref, nsd_ref), rate_matrix, decay_coef,
-    )
-    update(
-        nrm_ref[0:blk, :], fin_q[:, width3:], nrm_ref[blk : 2 * blk, :],
-        nrm_ref[2 * blk :, :],
-        (
-            nnrm_ref.at[pl.ds(0, blk)],
-            nnrm_ref.at[pl.ds(blk, blk)],
-            nnrm_ref.at[pl.ds(2 * blk, blk)],
-        ),
+        wn_ref[...], turned[0:count, 0:cols], fn_ref[...], sn_ref[...], (nn, nfn, nsn),
         rate_norm, 0.0,
     )
-    sent(seq_hops)
-    sent(dp_hops)
-    keep_act.wait()
-    keep_dx.wait()
+    for _, outward in moves:
+        outward.wait()
 
 
 def fused_device(
@@ -941,73 +1186,86 @@
     blocks = rows_all // SPAN
     far_n = seq_n * blocks
     keys_n = SPAN + local_len // SPAN * seq_n
-
-    def tall(rows_in):
-        return jnp.pad(rows_in.T, ((0, 0), (0, LANES - rows_in.shape[0])))
-
-    norm_pack = jnp.concatenate([tall(norm_params), tall(first_norm), tall(second_norm)], axis=0)
-    matrices = (w_qkv, w_out, w_up, w_down)
-    triples = [jax.ShapeDtypeStruct(w.shape, F32) for w in matrices for _ in range(3)]
-    nq, nu, nd = width3 + LANES, ff + width, width
-
-    def bufs(b, n, sends):
+    part_n = ff // nz
+    up_rows = nz * blk
+    half = width // 2
+
+    def bufs(b, n):
         cut = (n // 2) // LANES * LANES
         rest = n - cut
         taken = [pltpu.VMEM((nz, nx, b, cut), BF), pltpu.VMEM((ny, nz, b, rest), BF)]
         return [
+            *taken,
+            pltpu.VMEM((nz, b, n), BF),
             pltpu.VMEM((ny, nz, nx, b, n), BF),
-            *(taken if sends else []),
             *taken,
             pltpu.VMEM((nz, b, cut), BF),
             pltpu.VMEM((nz, b, rest), BF),
-            *([pltpu.VMEM((nz, b, n), BF)] if sends else []),
             pltpu.VMEM((nz - 1, b, n), BF),
         ]
 
     whole = pl.BlockSpec(memory_space=pltpu.VMEM)
     outside = pl.BlockSpec(memory_space=pl.ANY)
+    part_rows = up_rows + dblk
     outs = pl.pallas_call(
         layer_kernel,
         out_shape=[
             jax.ShapeDtypeStruct((rows_all, width), BF),
             jax.ShapeDtypeStruct((rows_all, width), F32),
+            jax.ShapeDtypeStruct(w_qkv.shape, F32),
+            jax.ShapeDtypeStruct(w_out.shape, F32),
+            jax.ShapeDtypeStruct(w_up.shape, F32),
+            jax.ShapeDtypeStruct(w_down.shape, F32),
+            jax.ShapeDtypeStruct((8, width), F32),
             jax.ShapeDtypeStruct((8, LANES), F32),
-            *triples,
-            jax.ShapeDtypeStruct(norm_pack.shape, F32),
         ],
-        in_specs=[pl.BlockSpec(memory_space=pltpu.SMEM), outside, outside] + [whole] * 13,
-        out_specs=[outside, outside] + [whole] * 14,
+        in_specs=[pl.BlockSpec(memory_space=pltpu.SMEM), outside, outside] + [whole] * 5,
+        out_specs=[outside, outside] + [whole] * 6,
         scratch_shapes=[
-            pltpu.VMEM((ny, nc, nz, nx, blk, nq), BF),
-            pltpu.VMEM((ny, nc, nz, nx, blk, nu), BF),
-            pltpu.VMEM((ny, nc, nz, nx, dblk, nd), BF),
+            pltpu.VMEM((ny, nc, nz, nx, blk, 2 * width + LANES), BF),
+            pltpu.VMEM((ny, nc, nz, nx, blk, 2 * width), BF),
+            pltpu.VMEM((ny, nc, nz, nx, blk, ff), BF),
+            pltpu.VMEM((ny, nc, nz, nx, dblk, width), BF),
             pltpu.VMEM((rows_all, width3), BF),
             pltpu.VMEM((rows_all, width), BF),
             pltpu.VMEM((blocks, width // LANES, keys_n, 2 * SPAN), BF),
-            pltpu.VMEM((ny, nc, nz, nx, blk, nq), F32),
-            pltpu.VMEM((ny, nc, nz, nx, blk, nu), F32),
-            pltpu.VMEM((width, ff), F32),
-            pltpu.VMEM((ny, nz, nx, dblk, nd), F32),
-            *bufs(blk, nq, False),
-            *bufs(blk, nu, True),
-            *bufs(dblk, nd, True),
+            pltpu.VMEM((ny, nc, nz, nx, blk, width3), F32),
+            pltpu.VMEM((ny, nc, nz, nx, blk, width), F32),
+            pltpu.VMEM((rows_all, width), F32),
+            pltpu.VMEM((rows_all, width), BF),
+            pltpu.VMEM((width, rows_all), BF),
+            pltpu.VMEM((width, rows_all), BF),
+            pltpu.VMEM((rows_all, part_n), BF),
+            pltpu.VMEM((rows_all, part_n), BF),
+            pltpu.VMEM((ny, nx, part_rows, width), F32),
+            pltpu.VMEM((ny, nx, part_rows, width), BF),
+            pltpu.VMEM((nz, ny, nx, part_rows, width), BF),
+            pltpu.VMEM((nx, part_rows, half), BF),
+            pltpu.VMEM((ny, part_rows, half), BF),
+            pltpu.VMEM((nz, nx, part_rows, half), BF),
+            pltpu.VMEM((nz, ny, part_rows, half), BF),
+            pltpu.VMEM((nz, part_rows, half), BF),
+            pltpu.VMEM((nz, part_rows, half), BF),
+            pltpu.VMEM((nz, nz, blk, width), BF),
+            pltpu.VMEM((nz - 1, nz, blk, width), BF),
+            pltpu.VMEM((nz, blk, width), F32),
+            pltpu.VMEM((nz, dblk, width), F32),
+            pltpu.VMEM((nz, dblk, width), BF),
+            pltpu.VMEM((nz - 1, dblk, width), BF),
+            *bufs(blk, width3),
+            *bufs(blk, width),
             pltpu.VMEM((seq_n, blocks, 2 * width), BF),
             pltpu.VMEM((far_n, 2 * width), BF),
             pltpu.VMEM((far_n, 2 * width), F32),
             pltpu.VMEM((seq_n, blocks, 2 * width), BF),
             pltpu.VMEM((seq_n - 1, blocks, 2 * width), BF),
-            pltpu.VMEM((blocks, 2 * width), F32),
+            pltpu.VMEM((blocks, width), F32),
+            pltpu.VMEM((blocks, width), F32),
             pltpu.VMEM((8, width), F32),
             pltpu.VMEM((4, 8, width), F32),
-            pltpu.VMEM((TILE, TILE), BF),
-            pltpu.VMEM((TILE, TILE), BF),
-            pltpu.VMEM((TILE, width), BF),
-            pltpu.VMEM((width, TILE), BF),
-            pltpu.VMEM((width, TILE), BF),
-            pltpu.VMEM((TILE, width), F32),
-            pltpu.VMEM((blk, nq), F32),
-            pltpu.VMEM((blk, nu), F32),
-            pltpu.VMEM((dblk, nd), F32),
+            pltpu.VMEM((LANES, LANES), F32),
+            pltpu.VMEM((seq_n, 8, width), F32),
+            pltpu.VMEM((dp_n, 8, width), F32),
             pltpu.VMEM((seq_n, 8, LANES), F32),
             pltpu.VMEM((dp_n, 8, LANES), F32),
             pltpu.VMEM((rows_all, width), BF),
@@ -1024,17 +1282,34 @@
         lengths,
         tokens.reshape(rows_all, width),
         cotangent.reshape(rows_all, width),
-        w_qkv, w_out, w_up, w_down, norm_pack,
-        first_qkv, first_out, first_up, first_down,
-        second_qkv, second_out, second_up, second_down,
-    )
-    act, grad, gnorm = outs[:3]
-    new_pack = outs[15]
-    count = norm_params.shape[0]
-    norms = [new_pack[k * blk : (k + 1) * blk, 0:count].T for k in range(3)]
+        w_qkv, w_out, w_up, w_down, norm_params,
+    )
+    weights = (w_qkv, w_out, w_up, w_down, norm_params)
+    new = pl.pallas_call(
+        update_kernel,
+        out_shape=[
+            jax.ShapeDtypeStruct((rows_all, width), BF),
+            jax.ShapeDtypeStruct((rows_all, width), F32),
+            jax.ShapeDtypeStruct((1, 1), F32),
+            *(jax.ShapeDtypeStruct(w.shape, F32) for w in weights for _ in range(3)),
+        ],
+        in_specs=[outside, outside] + [whole] * 21,
+        out_specs=[outside, outside] + [whole] * 16,
+        scratch_shapes=[
+            pltpu.VMEM((rows_all, width), BF),
+            pltpu.VMEM((rows_all, width), F32),
+            pltpu.SemaphoreType.DMA((8,)),
+            pltpu.SemaphoreType.DMA((8,)),
+        ],
+        compiler_params=pltpu.CompilerParams(vmem_limit_bytes=64 * 1024 * 1024 - 65536),
+    )(
+        outs[0], outs[1], outs[7], *outs[2:7], *weights,
+        first_qkv, first_out, first_up, first_down, first_norm,
+        second_qkv, second_out, second_up, second_down, second_norm,
+    )
     return (
-        act.reshape(tokens.shape), grad.reshape(tokens.shape), gnorm[0, 0],
-        *outs[3:15], *norms,
+        new[0].reshape(tokens.shape), new[1].reshape(tokens.shape), new[2].reshape(()),
+        *new[3:],
     )
 
 

time: 210 us -> 171 us (0.81)
  local copies, waits for them, and re-layouts: 19.1 us -> 0 us
  Pallas kernels: 189 us -> 170 us
    pallas_call x1, Pallas kernels: 189 us -> 162 us  [fused_device(): pl.pallas_call(layer_kernel, out_shape=[jax.ShapeDtypeStruct((rows_all, w...]
    unnamed x46 -> x0, local copies, waits for them, and re-layouts: 17.2 us -> none
    pallas_call x0 -> x1, Pallas kernels: none -> 7.93 us  [fused_device(): pl.pallas_call(update_kernel, out_shape=[jax.ShapeDtypeStruct((rows_all,...]
where the time goes in v2:
time: 171 us
  Pallas kernels  170 us (99%)
    pallas_call x1, Pallas kernels, fused_device(): pl.pallas_call(layer_kernel, out_shape=[jax.ShapeDtypeStruct((rows_all, w...  162 us
    pallas_call x1, Pallas kernels, fused_device(): pl.pallas_call(update_kernel, out_shape=[jax.ShapeDtypeStruct((rows_all,...  7.93 us

profile of v2, /device:TPU:0, one launch (start us, length us, event | category | flops | bytes accessed | tf_op | source)
XLA Modules:
  0.0 171.1 jit_solution(5014354562321010167)
XLA Ops:
  0.7 162.4 %shard_map.313 = (bf16[2048,512]{1,0:T(8,128)(2,1)}, f32[2048,512]{1,0:T(8,128)}, f32[16,1536]{1,0:T(8,128)}, f32[16,512]{1,0:T(8,128)}, f32[16,2048]{1,0:T(8,12...) custom-call(s32[8]{0:T(128)} %len_ref.1, bf16[2048,512]{1,0:T(8,128)(2,1)} %bitcast.5, ...), custom_call_target="tpu_custom_call" | custom-call | tf_op jit(solution)/shard_map/pallas_call | solution.py:1210
  163.0 7.9 %shard_map.314 = (bf16[2048,512]{1,0:T(8,128)(2,1)}, f32[2048,512]{1,0:T(8,128)}, f32[1,1]{1,0:T(1,128)}, f32[16,1536]{1,0:T(8,128)}, f32[16,1536]{1,0:T(8,128)}...) custom-call(bf16[2048,512]{1,0:T(8,128)(2,1)} %get-tuple-element.44., ...), custom_call_target="tpu_custom_call" | custom-call | tf_op jit(solution)/shard_map/pallas_call | solution.py:1288

commit v3 on v2

--- a/solution.py
+++ b/solution.py
@@ -305,7 +305,7 @@
 def layer_kernel(
     len_ref, x_any, dy_any, wq_ref, wo_ref, wu_ref, wd_ref, nrm_ref,
     act_any, dx_any, fin_q, fin_o, fin_u, fin_d, norm_sum, total_ref,
-    bkv, bqo, bu, bd, qkv, mix, prob, gq, go, yacc, h2_s, ht_s, dyt_s, act_s, dup_s,
+    bkv, bqo, bu, bd, qkv, mix, prob, dscore_s, gq, go, yacc, h2_s, ht_s, dyt_s, act_s, dup_s,
     own_p, s1p, r1p, s2ap, s2bp, r2ap, r2bp, r3ap, r3bp, s4p, r4p, fin_p, keep_d, s5d, r5d,
     s2aq, s2bq, s3q, r1q, r2aq, r2bq, r3aq, r3bq, r4q,
     s2ao, s2bo, s3o, r1o, r2ao, r2bo, r3ao, r3bo, r4o,
@@ -328,7 +328,7 @@
     per_tile = TILE // SPAN
     pairs = width // LANES
     part_n = ff // nz
-    half_tile = TILE // 2
+    ffn_rows = 2 * TILE
     dp_i = lax.axis_index("dp")
     sq_i = lax.axis_index("seq")
     y, c = dp_i // nc, dp_i % nc
@@ -480,7 +480,6 @@
     start(direct_u)
     start(direct_d)
     nacc[...] = jnp.zeros_like(nacc)
-    pool_grad[...] = jnp.zeros_like(pool_grad)
     arrived(hops_kv[0])
     start(hops_kv[1])
     load_dy.wait()
@@ -586,46 +585,62 @@
         far_cols = pl.ds(cols.start - width, cols.size)
         return jnp.concatenate([qkv[near_rows, cols], pool_far[far_rows, far_cols]], axis=0)
 
-    def diagonal(stacked):
-        return jnp.concatenate(
-            [stacked[0:HEAD_DIM, 0:SPAN], stacked[HEAD_DIM:, SPAN:]], axis=0
-        ).T
-
-    def attend(block, carry):
-        for at, part, stage in (
-            (0, 1, 0), (3, 0, 1), (4, 2, 0), (7, 1, 1), (8, 3, 0), (12, 2, 1), (15, 3, 1)
+    def cols_of(third, pair):
+        return pl.ds(third * width + pair * LANES, LANES)
+
+    def by_head(rows_in, first, second):
+        return jnp.concatenate([rows_in * first, rows_in * second], axis=0)
+
+    units = [(sub, pair) for sub in range(spans_here) for pair in range(pairs)]
+    items = blocks // spans_here
+
+    def rows_of(item, sub):
+        return pl.ds(pl.multiple_of(item * local_len + sub * SPAN, SPAN), SPAN)
+
+    def far_of(item):
+        return pl.ds(pl.multiple_of(item * spans_all, spans_all), spans_all)
+
+    def attend(item):
+        for at, moves in (
+            (0, ((1, 0),)), (1, ((0, 1),)), (2, ((2, 0),)), (3, ((1, 1),)),
+            (4, ((3, 0),)), (6, ((2, 1),)), (7, ((3, 1),)),
         ):
 
-            @pl.when(block == at)
-            def _(part=part, stage=stage):
-                pass_on(part, stage)
-
-        item = block // spans_here
-        sub = lax.rem(block, spans_here)
-        rows = pl.ds(pl.multiple_of(block * SPAN, SPAN), SPAN)
-        far_rows = pl.ds(pl.multiple_of(item * spans_all, spans_all), spans_all)
+            @pl.when(item == at)
+            def _(moves=moves):
+                for part, stage in moves:
+                    pass_on(part, stage)
+
+        far_rows = far_of(item)
         length = len_ref[item]
         key_at = lax.broadcasted_iota(jnp.int32, (keys_n, 2 * SPAN), 0)
         span_at = key_at - SPAN
-        mine = sq_i * spans_here + sub
-        near_ok = (key_at < SPAN) & (mine * SPAN + key_at < length)
-        far_ok = (key_at >= SPAN) & (span_at * SPAN < length) & (span_at != mine)
-        seen = near_ok | far_ok
-        for pair in range(pairs):
-            q2 = qkv[rows, pl.ds(pair * LANES, LANES)]
-            kk = both(rows, far_rows, pl.ds(width + pair * LANES, LANES))
-            vv = both(rows, far_rows, pl.ds(2 * width + pair * LANES, LANES))
-            qq = jnp.concatenate([q2 * query_a, q2 * query_b], axis=0)
-            score = jnp.where(seen, mm(kk, qq, NT), neg_fill)
-            top = jnp.max(score, axis=0, keepdims=True)
-            raised = jnp.exp(score - top)
-            share = (raised * (1.0 / jnp.sum(raised, axis=0, keepdims=True))).astype(BF)
-            prob[block, pair] = share
-            mixed = diagonal(mm(vv, share, TN))
-            mix[rows, pl.ds(pair * LANES, LANES)] = mixed.astype(BF)
-        return carry
-
-    lax.fori_loop(0, blocks, attend, 0)
+
+        def seen(sub):
+            mine = sq_i * spans_here + sub
+            near_ok = (key_at < SPAN) & (mine * SPAN + key_at < length)
+            return near_ok | ((key_at >= SPAN) & (span_at * SPAN < length) & (span_at != mine))
+
+        scores = []
+        for sub, pair in units:
+            rows = rows_of(item, sub)
+            kk = both(rows, far_rows, cols_of(1, pair))
+            scores.append(mm(kk, by_head(qkv[rows, cols_of(0, pair)], query_a, query_b), NT))
+        for (sub, pair), score in zip(units, scores):
+            score = jnp.where(seen(sub), score, neg_fill)
+            raised = jnp.exp(score - jnp.max(score, axis=0, keepdims=True))
+            share = raised * (1.0 / jnp.sum(raised, axis=0, keepdims=True))
+            prob[item * spans_here + sub, pair] = share.astype(BF)
+        for sub in range(spans_here):
+            rows = rows_of(item, sub)
+            mixed = []
+            for pair in range(pairs):
+                vv = both(rows, far_rows, cols_of(2, pair))
+                stacked = mm(vv, prob[item * spans_here + sub, pair], TN)
+                mixed += [stacked[0:HEAD_DIM, 0:SPAN], stacked[HEAD_DIM:, SPAN:]]
+            mix[rows, :] = jnp.concatenate(mixed, axis=0).T.astype(BF)
+
+    each(items, attend)
     for group in (*hops_kv, *hops_qo, direct_u, direct_d, pool_hops):
         sent(group)
 
@@ -752,10 +767,9 @@
             def _():
                 part_second(part - 1)
 
-            rows = tile_rows(tile)
-            for piece in range(2):
-                lo = tile * TILE + piece * half_tile
-                some = pl.ds(pl.multiple_of(lo, half_tile), half_tile)
+            rows = pl.ds(pl.multiple_of(tile * ffn_rows, ffn_rows), ffn_rows)
+            for piece in range(ffn_rows // TILE):
+                some = tile_rows(tile * (ffn_rows // TILE) + piece)
                 up = mm(h2_s[some, :], w_up)
                 square = up * up
                 bent = jnp.tanh(up * (gelu_in + (gelu_in * gelu_cube) * square))
@@ -768,7 +782,7 @@
             yacc[rows, :] += mm(act_s[rows, :], w_down)
             dx_ref[rows, :] += mm(dup_s[rows, :], w_up, NT)
 
-        each(tiles, ffn_tile)
+        each(rows_all // ffn_rows, ffn_tile)
 
         @pl.when(part > 0)
         def _():
@@ -912,44 +926,49 @@
         part_fourth(nz - 1)
         start(down_hops)
 
-    def attend_back(block, carry):
+    def attend_back(item):
         for at, step in (
-            (0, last_third), (5, fourth_and_down), (6, red_o[1]), (10, red_o[2]), (14, red_o[3])
+            (0, last_third), (2, fourth_and_down), (3, red_o[1]), (5, red_o[2]), (7, red_o[3])
         ):
 
-            @pl.when(block == at)
+            @pl.when(item == at)
             def _(step=step):
                 step()
 
-        item = block // spans_here
-        rows = pl.ds(pl.multiple_of(block * SPAN, SPAN), SPAN)
-        far_rows = pl.ds(pl.multiple_of(item * spans_all, spans_all), spans_all)
+        far_rows = far_of(item)
+        dshares = []
+        for sub, pair in units:
+            rows = rows_of(item, sub)
+            vv = both(rows, far_rows, cols_of(2, pair))
+            dshares.append(mm(vv, by_head(mix[rows, cols_of(0, pair)], grad_a, grad_b), NT))
+        for (sub, pair), dshare in zip(units, dshares):
+            share = prob[item * spans_here + sub, pair].astype(F32)
+            inner = jnp.sum(share * dshare, axis=0, keepdims=True)
+            dscore_s[sub, pair] = (share * (dshare - inner)).astype(BF)
+        far_k, far_v = [0.0] * pairs, [0.0] * pairs
+        for sub in range(spans_here):
+            rows = rows_of(item, sub)
+            dqs = []
+            for pair in range(pairs):
+                dscore = dscore_s[sub, pair]
+                stacked = mm(both(rows, far_rows, cols_of(1, pair)), dscore, TN)
+                dqs += [stacked[0:HEAD_DIM, 0:SPAN], stacked[HEAD_DIM:, SPAN:]]
+                dk = mm(dscore, by_head(qkv[rows, cols_of(0, pair)], query_a, query_b))
+                dv = mm(
+                    prob[item * spans_here + sub, pair],
+                    by_head(mix[rows, cols_of(0, pair)], grad_a, grad_b),
+                )
+                qkv[rows, cols_of(1, pair)] = dk[0:SPAN].astype(BF)
+                qkv[rows, cols_of(2, pair)] = dv[0:SPAN].astype(BF)
+                far_k[pair] = far_k[pair] + dk[SPAN:]
+                far_v[pair] = far_v[pair] + dv[SPAN:]
+            dq = jnp.concatenate(dqs, axis=0).T * score_scale
+            qkv[rows, 0:width] = dq.astype(BF)
         for pair in range(pairs):
-            q_cols = pl.ds(pair * LANES, LANES)
-            k_cols = pl.ds(width + pair * LANES, LANES)
-            v_cols = pl.ds(2 * width + pair * LANES, LANES)
-            q2 = qkv[rows, q_cols]
-            do2 = mix[rows, q_cols]
-            kk = both(rows, far_rows, k_cols)
-            vv = both(rows, far_rows, v_cols)
-            qq = jnp.concatenate([q2 * query_a, q2 * query_b], axis=0)
-            dd = jnp.concatenate([do2 * grad_a, do2 * grad_b], axis=0)
-            share = prob[block, pair]
-            share_f = share.astype(F32)
-            dshare = mm(vv, dd, NT)
-            inner = jnp.sum(share_f * dshare, axis=0, keepdims=True)
-            dscore = (share_f * (dshare - inner)).astype(BF)
-            dq = diagonal(mm(kk, dscore, TN)) * score_scale
-            dk = mm(dscore, qq)
-            dv = mm(share, dd)
-            qkv[rows, q_cols] = dq.astype(BF)
-            qkv[rows, k_cols] = dk[0:SPAN].astype(BF)
-            qkv[rows, v_cols] = dv[0:SPAN].astype(BF)
-            pool_grad[far_rows, q_cols] += dk[SPAN:]
-            pool_grad[far_rows, pl.ds(width + pair * LANES, LANES)] += dv[SPAN:]
-        return carry
-
-    lax.fori_loop(0, blocks, attend_back, 0)
+            pool_grad[far_rows, cols_of(0, pair)] = far_k[pair]
+            pool_grad[far_rows, cols_of(1, pair)] = far_v[pair]
+
+    each(items, attend_back)
 
     back_row = lax.broadcasted_iota(jnp.int32, (far_n, far_n), 0)
     back_col = lax.broadcasted_iota(jnp.int32, (far_n, far_n), 1)
@@ -1229,6 +1248,7 @@
             pltpu.VMEM((rows_all, width3), BF),
             pltpu.VMEM((rows_all, width), BF),
             pltpu.VMEM((blocks, width // LANES, keys_n, 2 * SPAN), BF),
+            pltpu.VMEM((local_len // SPAN, width // LANES, keys_n, 2 * SPAN), BF),
             pltpu.VMEM((ny, nc, nz, nx, blk, width3), F32),
             pltpu.VMEM((ny, nc, nz, nx, blk, width), F32),
             pltpu.VMEM((rows_all, width), F32),

time: 171 us -> 159 us (0.930)
  Pallas kernels: 170 us -> 158 us
    pallas_call x1, Pallas kernels: 162 us -> 150 us  [fused_device(): pl.pallas_call(layer_kernel, out_shape=[jax.ShapeDtypeStruct((rows_all, w...]
where the time goes in v3:
time: 159 us
  Pallas kernels  158 us (99%)
    pallas_call x1, Pallas kernels, fused_device(): pl.pallas_call(layer_kernel, out_shape=[jax.ShapeDtypeStruct((rows_all, w...  150 us
    pallas_call x1, Pallas kernels, fused_device(): pl.pallas_call(update_kernel, out_shape=[jax.ShapeDtypeStruct((rows_all,...  7.93 us

profile of v3, /device:TPU:0, one launch (start us, length us, event | category | flops | bytes accessed | tf_op | source)
XLA Modules:
  0.0 158.6 jit_solution(2970919619445243535)
XLA Ops:
  0.7 149.8 %shard_map.313 = (bf16[2048,512]{1,0:T(8,128)(2,1)}, f32[2048,512]{1,0:T(8,128)}, f32[16,1536]{1,0:T(8,128)}, f32[16,512]{1,0:T(8,128)}, f32[16,2048]{1,0:T(8,12...) custom-call(s32[8]{0:T(128)} %len_ref.1, bf16[2048,512]{1,0:T(8,128)(2,1)} %bitcast.5, ...), custom_call_target="tpu_custom_call" | custom-call | tf_op jit(solution)/shard_map/pallas_call | solution.py:1229
  150.5 7.9 %shard_map.314 = (bf16[2048,512]{1,0:T(8,128)(2,1)}, f32[2048,512]{1,0:T(8,128)}, f32[1,1]{1,0:T(1,128)}, f32[16,1536]{1,0:T(8,128)}, f32[16,1536]{1,0:T(8,128)}...) custom-call(bf16[2048,512]{1,0:T(8,128)(2,1)} %get-tuple-element.44., ...), custom_call_target="tpu_custom_call" | custom-call | tf_op jit(solution)/shard_map/pallas_call | solution.py:1308

commit v4 on v3

--- a/solution.py
+++ b/solution.py
@@ -277,8 +277,8 @@
 NN = (((1,), (0,)), ((), ()))
 NT = (((1,), (1,)), ((), ()))
 TN = (((0,), (0,)), ((), ()))
-GATHER, SPREAD, PARTS, DOWN, OUTER, INNER, POOL, POOLBACK = 0, 22, 62, 94, 97, 105, 113, 120
-NORM_SEQ, NORM_DP, SQUARE_SEQ, SQUARE_DP, COPIES = 127, 134, 137, 144, 147
+GATHER, SPREAD, PARTS, DOWN, OUTER, INNER, POOL, POOLBACK = 0, 22, 62, 94, 97, 105, 121, 128
+NORM_SEQ, NORM_DP, SQUARE_SEQ, SQUARE_DP, COPIES = 135, 142, 145, 152, 155
 
 
 def mm(left, right, dims=NN):
@@ -305,9 +305,10 @@
 def layer_kernel(
     len_ref, x_any, dy_any, wq_ref, wo_ref, wu_ref, wd_ref, nrm_ref,
     act_any, dx_any, fin_q, fin_o, fin_u, fin_d, norm_sum, total_ref,
-    bkv, bqo, bu, bd, qkv, mix, prob, dscore_s, gq, go, yacc, h2_s, ht_s, dyt_s, act_s, dup_s,
-    own_p, s1p, r1p, s2ap, s2bp, r2ap, r2bp, r3ap, r3bp, s4p, r4p, fin_p, keep_d, s5d, r5d,
+    bkv, bqo, bu, bd, qkv, mix, prob, gq, go, yacc, h2_s, ht_s, dyt_s, act_s, dup_s,
+    own_p, kept_p, s1p, r1p, s2ap, s2bp, r2ap, r2bp, r3ap, r3bp, s4p, r4p, fin_p, keep_d, s5d, r5d,
     s2aq, s2bq, s3q, r1q, r2aq, r2bq, r3aq, r3bq, r4q,
+    s2ak, s2bk, s3k, r1k, r2ak, r2bk, r3ak, r3bk, r4k,
     s2ao, s2bo, s3o, r1o, r2ao, r2bo, r3ao, r3bo, r4o,
     pool_all, pool_far, pool_grad, pool_send, pool_recv, live_sum, spread_w,
     nrow, nacc, ntall, norm_seq, norm_dp, psq, psd, x_ref, dy_ref, dx_ref,
@@ -375,7 +376,13 @@
 
         lax.fori_loop(0, count, step, 0)
 
+    def flat(count, body):
+        for index in range(count):
+            body(index)
+
     def tile_rows(tile):
+        if isinstance(tile, int):
+            return pl.ds(tile * TILE, TILE)
         return pl.ds(pl.multiple_of(tile * TILE, TILE), TILE)
 
     load_x = pltpu.make_async_copy(x_any, x_ref, local_sem.at[0])
@@ -535,14 +542,14 @@
         for part in (1, 2):
             qkv[rows, pl.ds(part * width, width)] = mm(h1, w_qkv(part)).astype(BF)
 
-        @pl.when(tile == 3)
-        def _():
+        if tile == 3:
             arrived(hops_qo[2])
             start(hops_qo[3])
-
         return pooled + mm(live_pick(tile), qkv[rows, width:])
 
-    pooled = lax.fori_loop(0, tiles, kv_tile, jnp.zeros((blocks, 2 * width), F32))
+    pooled = jnp.zeros((blocks, 2 * width), F32)
+    for index in range(tiles):
+        pooled = kv_tile(index, pooled)
     block_col = lax.broadcasted_iota(jnp.int32, (blocks, 1), 0)
     length_col = jnp.zeros((blocks, 1), jnp.int32)
     for i in range(blocks // spans_here):
@@ -562,7 +569,7 @@
         rows = tile_rows(tile)
         qkv[rows, 0:width] = mm(h2_s[rows, :], w_qkv(0)).astype(BF)
 
-    each(tiles, q_tile)
+    flat(tiles, q_tile)
     arrived(pool_hops)
 
     far_n = seq_n * blocks
@@ -662,7 +669,7 @@
         h2_s[rows, :] = h2.astype(BF)
         ht_s[:, rows] = h2.T.astype(BF)
 
-    each(tiles, ffn_open)
+    flat(tiles, ffn_open)
 
     half_cols = width // 2
     one_p, two_p = pl.ds(0, half_cols), pl.ds(half_cols, half_cols)
@@ -670,15 +677,16 @@
 
     def part_hops(part):
         base = PARTS + part * 8
+        slot = part % 2
         return (
-            [hop(s1p, r1p.at[part], base, twin)],
+            [hop(s1p, r1p.at[slot], base, twin)],
             [
-                hop(s1p.at[1 - y, :, :, one_p], r2ap.at[part], base + 1, over_y),
-                hop(s1p.at[:, 1 - x, :, two_p], r2bp.at[part], base + 2, over_x),
+                hop(s1p.at[1 - y, :, :, one_p], r2ap.at[slot], base + 1, over_y),
+                hop(s1p.at[:, 1 - x, :, two_p], r2bp.at[slot], base + 2, over_x),
             ],
             [
-                hop(s2ap.at[1 - x], r3ap.at[part], base + 3, over_x),
-                hop(s2bp.at[1 - y], r3bp.at[part], base + 4, over_y),
+                hop(s2ap.at[1 - x], r3ap.at[slot], base + 3, over_x),
+                hop(s2bp.at[1 - y], r3bp.at[slot], base + 4, over_y),
             ],
             [
                 hop(
@@ -714,7 +722,7 @@
 
         def add(index):
             yy, xx = index // nx, index % nx
-            total = own_p[yy, xx] + r1p[part, yy, xx].astype(F32)
+            total = own_p[yy, xx] + r1p[part % 2, yy, xx].astype(F32)
             own_p[yy, xx] = total
             s1p[yy, xx] = total.astype(BF)
 
@@ -726,25 +734,26 @@
         arrived(hops[1])
         sent(hops[1])
         for xx in range(nx):
-            total = own_p[y, xx, :, one_p] + r2ap[part, xx].astype(F32)
+            total = own_p[y, xx, :, one_p] + r2ap[part % 2, xx].astype(F32)
             own_p[y, xx, :, one_p] = total
             s2ap[xx] = total.astype(BF)
         for yy in range(ny):
-            total = own_p[yy, x, :, two_p] + r2bp[part, yy].astype(F32)
+            total = own_p[yy, x, :, two_p] + r2bp[part % 2, yy].astype(F32)
             own_p[yy, x, :, two_p] = total
             s2bp[yy] = total.astype(BF)
+        kept_p[...] = own_p[y, x]
         start(hops[2])
 
     def part_fourth(part):
         hops = part_hops(part)
         arrived(hops[2])
         sent(hops[2])
-        own_p[y, x, :, one_p] += r3ap[part].astype(F32)
-        own_p[y, x, :, two_p] += r3bp[part].astype(F32)
+        kept_p[:, one_p] += r3ap[part % 2].astype(F32)
+        kept_p[:, two_p] += r3bp[part % 2].astype(F32)
         for zz in range(nz):
-            s4p[part, zz] = own_p[y, x, zz * blk : (zz + 1) * blk].astype(BF)
-        fin_p[part] = own_p[y, x, pl.ds(pl.multiple_of(z * blk, blk), blk)]
-        down = own_p[y, x, up_rows:]
+            s4p[part, zz] = kept_p[zz * blk : (zz + 1) * blk].astype(BF)
+        fin_p[part] = kept_p[pl.ds(pl.multiple_of(z * blk, blk), blk)]
+        down = kept_p[up_rows:]
         keep_d[part] = down
         s5d[part] = down.astype(BF)
         start(hops[3])
@@ -784,27 +793,27 @@
 
         each(rows_all // ffn_rows, ffn_tile)
 
+        @pl.when(part > 1)
+        def _():
+            part_fourth(part - 2)
+
+        gq[:, :, :, :, :, 0:part_n] = mm(dyt_s[...], act_s[...]).reshape(go.shape)
+        go[...] = mm(ht_s[...], dup_s[...]).reshape(go.shape)
+
         @pl.when(part > 0)
         def _():
             part_third(part - 1)
 
-        gq[:, :, :, :, :, 0:part_n] = mm(dyt_s[...], act_s[...]).reshape(go.shape)
-        go[...] = mm(ht_s[...], dup_s[...]).reshape(go.shape)
-
-        @pl.when(part > 0)
-        def _():
-            part_fourth(part - 1)
-
         part_first(part)
         return carry
 
     lax.fori_loop(0, nz, ffn_part, 0)
 
     def ffn_close(tile):
-        @pl.when(tile == 1)
-        def _():
+        if tile == 2:
             part_second(nz - 1)
-
+        if tile == 3:
+            part_fourth(nz - 2)
         rows = tile_rows(tile)
         _, hat, scale = second_norm(rows)
         dh2 = dx_ref[rows, :]
@@ -818,14 +827,15 @@
         ht_s[:, rows] = mix[rows, :].astype(F32).T.astype(BF)
         mix[rows, :] = mm(dz, w_out, NT).astype(BF)
 
-    each(tiles, ffn_close)
+    flat(tiles, ffn_close)
     keep_act.start()
     for part in range(nz):
         for group in spread_hops(part):
             sent(group)
     go[...] = mm(ht_s[...], act_s[...]).reshape(go.shape)
 
-    def reduce_steps(full, s1, r1, s2a, s2b, r2a, r2b, r3a, r3b, s3, r4, fin, base):
+    def reduce_steps(full, cols, s1, r1, s2a, s2b, r2a, r2b, r3a, r3b, s3, r4, fin, base):
+        full = full.at[:, :, :, :, :, cols]
         own = full.at[:, c]
         n = s1.shape[4]
         cut = (n // 2) // LANES * LANES
@@ -902,20 +912,25 @@
             total = own[y, z, x]
             for step in range(nz - 1):
                 total = total + r4[step].astype(F32)
-            fin[...] = total
+            fin[:, cols] = total
             sent(hop2)
             sent(hop3)
             sent(hop4)
 
         return stage1, stage2, stage3, stage4, stage5
 
+    cols_q, cols_kv = pl.ds(0, width), pl.ds(width, 2 * width)
     red_o = reduce_steps(
-        go, bu.at[:, 0, :, :, :, pl.ds(0, width)], r1o, s2ao, s2bo, r2ao, r2bo, r3ao, r3bo, s3o,
+        go, cols_q, bu.at[:, 0, :, :, :, cols_q], r1o, s2ao, s2bo, r2ao, r2bo, r3ao, r3bo, s3o,
         r4o, fin_o, OUTER,
     )
     red_q = reduce_steps(
-        gq, bu.at[:, 1, :, :, :, pl.ds(0, width3)], r1q, s2aq, s2bq, r2aq, r2bq, r3aq, r3bq,
+        gq, cols_q, bu.at[:, 1, :, :, :, cols_q], r1q, s2aq, s2bq, r2aq, r2bq, r3aq, r3bq,
         s3q, r4q, fin_q, INNER,
+    )
+    red_kv = reduce_steps(
+        gq, cols_kv, bu.at[:, 1, :, :, :, cols_kv], r1k, s2ak, s2bk, r2ak, r2bk, r3ak, r3bk,
+        s3k, r4k, fin_q, INNER + 8,
     )
     red_o[0]()
 
@@ -928,7 +943,7 @@
 
     def attend_back(item):
         for at, step in (
-            (0, last_third), (2, fourth_and_down), (3, red_o[1]), (5, red_o[2]), (7, red_o[3])
+            (0, red_o[1]), (1, last_third), (3, fourth_and_down), (4, red_o[2]), (7, red_o[3])
         ):
 
             @pl.when(item == at)
@@ -941,27 +956,26 @@
             rows = rows_of(item, sub)
             vv = both(rows, far_rows, cols_of(2, pair))
             dshares.append(mm(vv, by_head(mix[rows, cols_of(0, pair)], grad_a, grad_b), NT))
+        far_k, far_v = [0.0] * pairs, [0.0] * pairs
         for (sub, pair), dshare in zip(units, dshares):
-            share = prob[item * spans_here + sub, pair].astype(F32)
+            rows, at = rows_of(item, sub), item * spans_here + sub
+            share = prob[at, pair]
+            dv = mm(share, by_head(mix[rows, cols_of(0, pair)], grad_a, grad_b))
+            qkv[rows, cols_of(2, pair)] = dv[0:SPAN].astype(BF)
+            far_v[pair] = far_v[pair] + dv[SPAN:]
+            share = share.astype(F32)
             inner = jnp.sum(share * dshare, axis=0, keepdims=True)
-            dscore_s[sub, pair] = (share * (dshare - inner)).astype(BF)
-        far_k, far_v = [0.0] * pairs, [0.0] * pairs
+            prob[at, pair] = (share * (dshare - inner)).astype(BF)
         for sub in range(spans_here):
             rows = rows_of(item, sub)
             dqs = []
             for pair in range(pairs):
-                dscore = dscore_s[sub, pair]
+                dscore = prob[item * spans_here + sub, pair]
                 stacked = mm(both(rows, far_rows, cols_of(1, pair)), dscore, TN)
                 dqs += [stacked[0:HEAD_DIM, 0:SPAN], stacked[HEAD_DIM:, SPAN:]]
                 dk = mm(dscore, by_head(qkv[rows, cols_of(0, pair)], query_a, query_b))
-                dv = mm(
-                    prob[item * spans_here + sub, pair],
-                    by_head(mix[rows, cols_of(0, pair)], grad_a, grad_b),
-                )
                 qkv[rows, cols_of(1, pair)] = dk[0:SPAN].astype(BF)
-                qkv[rows, cols_of(2, pair)] = dv[0:SPAN].astype(BF)
                 far_k[pair] = far_k[pair] + dk[SPAN:]
-                far_v[pair] = far_v[pair] + dv[SPAN:]
             dq = jnp.concatenate(dqs, axis=0).T * score_scale
             qkv[rows, 0:width] = dq.astype(BF)
         for pair in range(pairs):
@@ -1001,6 +1015,9 @@
         gq[:, :, :, :, :, cols] = mm(ht_s[...], qkv[:, cols]).reshape(
             ny, nc, nz, nx, blk, width
         )
+        if part == 0:
+            red_q[0]()
+    red_q[1]()
     for part in range(nz):
         arrived(part_hops(part)[3])
         total = fin_p[part]
@@ -1033,17 +1050,19 @@
         gq[:, :, :, :, :, cols] += mm(left, right[:, part * width : (part + 1) * width], TN).reshape(
             ny, nc, nz, nx, blk, width
         )
-    red_q[0]()
+    red_kv[0]()
     far_two = jnp.concatenate([far_hi, far_lo], axis=0)
     both_far = mm(far_two[:, 0:width], w_qkv(1), NT) + mm(far_two[:, width:], w_qkv(2), NT)
     spread_w[...] = both_far[0:blocks] + both_far[blocks:]
 
     def last_tile(tile):
-        for at, step in ((1, red_q[1]), (3, red_q[2])):
-
-            @pl.when(tile == at)
-            def _(step=step):
-                step()
+        @pl.when(tile == 1)
+        def _():
+            red_kv[1]()
+
+        @pl.when(tile == 2)
+        def _():
+            red_q[2]()
 
         rows = tile_rows(tile)
         hat, scale, _ = first_norm(rows)
@@ -1078,6 +1097,7 @@
         for step in range(1, dp_n)
     ]
     start(norm_hops)
+    red_kv[2]()
     red_q[3]()
     arrived(norm_hops)
     total = norm_seq[0]
@@ -1085,6 +1105,8 @@
         total = total + norm_seq[k]
     norm_dp[dp_i] = total
     start(norm_hops_dp)
+    red_kv[3]()
+    red_q[4]()
 
     def partial(values_in):
         squares = fold_rows(values_in * values_in)
@@ -1093,7 +1115,7 @@
         )
 
     early = partial(fin_u[...]) + partial(fin_d[...]) + partial(fin_o[...])
-    red_q[4]()
+    red_kv[4]()
     psq[sq_i] = early + partial(fin_q[...])
     seq_hops = [
         hop(psq.at[sq_i], psq.at[sq_i], SQUARE_SEQ + step - 1, (dp_i, seq_peer(step)))
@@ -1248,7 +1270,6 @@
             pltpu.VMEM((rows_all, width3), BF),
             pltpu.VMEM((rows_all, width), BF),
             pltpu.VMEM((blocks, width // LANES, keys_n, 2 * SPAN), BF),
-            pltpu.VMEM((local_len // SPAN, width // LANES, keys_n, 2 * SPAN), BF),
             pltpu.VMEM((ny, nc, nz, nx, blk, width3), F32),
             pltpu.VMEM((ny, nc, nz, nx, blk, width), F32),
             pltpu.VMEM((rows_all, width), F32),
@@ -1258,21 +1279,23 @@
             pltpu.VMEM((rows_all, part_n), BF),
             pltpu.VMEM((rows_all, part_n), BF),
             pltpu.VMEM((ny, nx, part_rows, width), F32),
+            pltpu.VMEM((part_rows, width), F32),
             pltpu.VMEM((ny, nx, part_rows, width), BF),
-            pltpu.VMEM((nz, ny, nx, part_rows, width), BF),
+            pltpu.VMEM((2, ny, nx, part_rows, width), BF),
             pltpu.VMEM((nx, part_rows, half), BF),
             pltpu.VMEM((ny, part_rows, half), BF),
-            pltpu.VMEM((nz, nx, part_rows, half), BF),
-            pltpu.VMEM((nz, ny, part_rows, half), BF),
-            pltpu.VMEM((nz, part_rows, half), BF),
-            pltpu.VMEM((nz, part_rows, half), BF),
+            pltpu.VMEM((2, nx, part_rows, half), BF),
+            pltpu.VMEM((2, ny, part_rows, half), BF),
+            pltpu.VMEM((2, part_rows, half), BF),
+            pltpu.VMEM((2, part_rows, half), BF),
             pltpu.VMEM((nz, nz, blk, width), BF),
             pltpu.VMEM((nz - 1, nz, blk, width), BF),
             pltpu.VMEM((nz, blk, width), F32),
             pltpu.VMEM((nz, dblk, width), F32),
             pltpu.VMEM((nz, dblk, width), BF),
             pltpu.VMEM((nz - 1, dblk, width), BF),
-            *bufs(blk, width3),
+            *bufs(blk, width),
+            *bufs(blk, 2 * width),
             *bufs(blk, width),
             pltpu.VMEM((seq_n, blocks, 2 * width), BF),
             pltpu.VMEM((far_n, 2 * width), BF),

time: 159 us -> 151 us (0.950)
  Pallas kernels: 158 us -> 150 us
    pallas_call x1, Pallas kernels: 150 us -> 142 us  [fused_device(): pl.pallas_call(layer_kernel, out_shape=[jax.ShapeDtypeStruct((rows_all, w...]
where the time goes in v4:
time: 151 us
  Pallas kernels  150 us (99%)
    pallas_call x1, Pallas kernels, fused_device(): pl.pallas_call(layer_kernel, out_shape=[jax.ShapeDtypeStruct((rows_all, w...  142 us
    pallas_call x1, Pallas kernels, fused_device(): pl.pallas_call(update_kernel, out_shape=[jax.ShapeDtypeStruct((rows_all,...  7.93 us

profile of v4, /device:TPU:0, one launch (start us, length us, event | category | flops | bytes accessed | tf_op | source)
XLA Modules:
  0.0 151.1 jit_solution(2758217395133344053)
XLA Ops:
  0.7 142.4 %shard_map.313 = (bf16[2048,512]{1,0:T(8,128)(2,1)}, f32[2048,512]{1,0:T(8,128)}, f32[16,1536]{1,0:T(8,128)}, f32[16,512]{1,0:T(8,128)}, f32[16,2048]{1,0:T(8,12...) custom-call(s32[8]{0:T(128)} %len_ref.1, bf16[2048,512]{1,0:T(8,128)(2,1)} %bitcast.5, ...), custom_call_target="tpu_custom_call" | custom-call | tf_op jit(solution)/shard_map/pallas_call | solution.py:1251
  143.0 7.9 %shard_map.314 = (bf16[2048,512]{1,0:T(8,128)(2,1)}, f32[2048,512]{1,0:T(8,128)}, f32[1,1]{1,0:T(1,128)}, f32[16,1536]{1,0:T(8,128)}, f32[16,1536]{1,0:T(8,128)}...) custom-call(bf16[2048,512]{1,0:T(8,128)(2,1)} %get-tuple-element.44., ...), custom_call_target="tpu_custom_call" | custom-call | tf_op jit(solution)/shard_map/pallas_call | solution.py:1331

commit v5 on v4

--- a/solution.py
+++ b/solution.py
@@ -484,11 +484,11 @@
     direct_d = direct(bd, GATHER + 19)
     start(hops_kv[0])
     start(hops_qo[0])
-    start(direct_u)
-    start(direct_d)
     nacc[...] = jnp.zeros_like(nacc)
     arrived(hops_kv[0])
     start(hops_kv[1])
+    start(direct_u)
+    start(direct_d)
     load_dy.wait()
 
     def turn_dy(tile):
@@ -502,6 +502,12 @@
     start(hops_qo[1])
     load_x.wait()
     each(tiles // 2, lambda tile: turn_dy(tile + tiles // 2))
+
+    def first_hat(tile):
+        rows = tile_rows(tile)
+        dx_ref[rows, :] = centered(x_ref[rows, :].astype(F32))[0]
+
+    each(tiles, first_hat)
     arrived(hops_kv[2])
     start(hops_kv[3])
     arrived(hops_qo[1])
@@ -537,7 +543,7 @@
 
     def kv_tile(tile, pooled):
         rows = tile_rows(tile)
-        _, _, h1 = first_norm(rows)
+        h1 = (dx_ref[rows, :] * nrow[0:1, :] + nrow[1:2, :]).astype(BF)
         h2_s[rows, :] = h1
         for part in (1, 2):
             qkv[rows, pl.ds(part * width, width)] = mm(h1, w_qkv(part)).astype(BF)
@@ -609,8 +615,7 @@
 
     def attend(item):
         for at, moves in (
-            (0, ((1, 0),)), (1, ((0, 1),)), (2, ((2, 0),)), (3, ((1, 1),)),
-            (4, ((3, 0),)), (6, ((2, 1),)), (7, ((3, 1),)),
+            (0, ((1, 0),)), (2, ((0, 1), (2, 0))), (4, ((3, 0),)), (7, ((1, 1),)),
         ):
 
             @pl.when(item == at)
@@ -661,6 +666,8 @@
         return x1, hat, scale
 
     def ffn_open(tile):
+        if tile == 2:
+            pass_on(2, 1)
         rows = tile_rows(tile)
         x1, hat, _ = second_norm(rows)
         yacc[rows, :] = x1
@@ -772,6 +779,10 @@
         w_down = bd[:, :, part].reshape(part_n, width)
 
         def ffn_tile(tile):
+            @pl.when((part == 0) & (tile == 1))
+            def _():
+                pass_on(3, 1)
+
             @pl.when((part > 0) & (tile == 1))
             def _():
                 part_second(part - 1)
@@ -1018,21 +1029,6 @@
         if part == 0:
             red_q[0]()
     red_q[1]()
-    for part in range(nz):
-        arrived(part_hops(part)[3])
-        total = fin_p[part]
-        for step in range(nz - 1):
-            total = total + r4p[step, part].astype(F32)
-        for group in range(dp_n):
-            at = (group * nz + part) * LANES
-            fin_u[:, at : at + LANES] = total[:, group * LANES : (group + 1) * LANES]
-    arrived(down_hops)
-    total = keep_d[z]
-    for step in range(nz - 1):
-        total = total + r5d[step].astype(F32)
-    fin_d[...] = total
-    red_o[4]()
-
     arrived(back_hops)
     pool_total = pool_send[sq_i].astype(F32)
     for step in range(seq_n - 1):
@@ -1099,6 +1095,21 @@
     start(norm_hops)
     red_kv[2]()
     red_q[3]()
+    for part in range(nz):
+        arrived(part_hops(part)[3])
+        total = fin_p[part]
+        for step in range(nz - 1):
+            total = total + r4p[step, part].astype(F32)
+        for group in range(dp_n):
+            at = (group * nz + part) * LANES
+            fin_u[:, at : at + LANES] = total[:, group * LANES : (group + 1) * LANES]
+    arrived(down_hops)
+    total = keep_d[z]
+    for step in range(nz - 1):
+        total = total + r5d[step].astype(F32)
+    fin_d[...] = total
+    red_o[4]()
+
     arrived(norm_hops)
     total = norm_seq[0]
     for k in range(1, seq_n):
@@ -1161,7 +1172,7 @@
     act_out, dx_out, norm_ref, nq, nfq, nsq, no, nfo, nso, nu, nfu, nsu, nd, nfd, nsd,
     nn, nfn, nsn, act_s, dx_s, sems_in, sems_out,
 ):
-    pieces = 4
+    pieces = 2
     piece = act_s.shape[0] // pieces
     moves = []
     for k in range(pieces):
@@ -1341,8 +1352,8 @@
         scratch_shapes=[
             pltpu.VMEM((rows_all, width), BF),
             pltpu.VMEM((rows_all, width), F32),
-            pltpu.SemaphoreType.DMA((8,)),
-            pltpu.SemaphoreType.DMA((8,)),
+            pltpu.SemaphoreType.DMA((4,)),
+            pltpu.SemaphoreType.DMA((4,)),
         ],
         compiler_params=pltpu.CompilerParams(vmem_limit_bytes=64 * 1024 * 1024 - 65536),
     )(

time: 151 us -> 147 us (0.974)
  Pallas kernels: 150 us -> 146 us
    pallas_call x1, Pallas kernels: 142 us -> 139 us  [fused_device(): pl.pallas_call(layer_kernel, out_shape=[jax.ShapeDtypeStruct((rows_all, w...]
where the time goes in v5:
time: 147 us
  Pallas kernels  146 us (99%)
    pallas_call x1, Pallas kernels, fused_device(): pl.pallas_call(layer_kernel, out_shape=[jax.ShapeDtypeStruct((rows_all, w...  139 us
    pallas_call x1, Pallas kernels, fused_device(): pl.pallas_call(update_kernel, out_shape=[jax.ShapeDtypeStruct((rows_all,...  7.14 us

profile of v5, /device:TPU:0, one launch (start us, length us, event | category | flops | bytes accessed | tf_op | source)
XLA Modules:
  0.0 147.1 jit_solution(10397815579975785213)
XLA Ops:
  0.7 139.1 %shard_map.313 = (bf16[2048,512]{1,0:T(8,128)(2,1)}, f32[2048,512]{1,0:T(8,128)}, f32[16,1536]{1,0:T(8,128)}, f32[16,512]{1,0:T(8,128)}, f32[16,2048]{1,0:T(8,12...) custom-call(s32[8]{0:T(128)} %len_ref.1, bf16[2048,512]{1,0:T(8,128)(2,1)} %bitcast.5, ...), custom_call_target="tpu_custom_call" | custom-call | tf_op jit(solution)/shard_map/pallas_call | solution.py:1262
  139.8 7.1 %shard_map.314 = (bf16[2048,512]{1,0:T(8,128)(2,1)}, f32[2048,512]{1,0:T(8,128)}, f32[1,1]{1,0:T(1,128)}, f32[16,1536]{1,0:T(8,128)}, f32[16,1536]{1,0:T(8,128)}...) custom-call(bf16[2048,512]{1,0:T(8,128)(2,1)} %get-tuple-element.44., ...), custom_call_target="tpu_custom_call" | custom-call | tf_op jit(solution)/shard_map/pallas_call | solution.py:1342

commit v6 on v5

--- a/solution.py
+++ b/solution.py
@@ -613,46 +613,48 @@
     def far_of(item):
         return pl.ds(pl.multiple_of(item * spans_all, spans_all), spans_all)
 
-    def attend(item):
+    def attend(two):
         for at, moves in (
-            (0, ((1, 0),)), (2, ((0, 1), (2, 0))), (4, ((3, 0),)), (7, ((1, 1),)),
+            (0, ((1, 0),)), (1, ((0, 1), (2, 0))), (2, ((3, 0),)), (3, ((1, 1),)),
         ):
 
-            @pl.when(item == at)
+            @pl.when(two == at)
             def _(moves=moves):
                 for part, stage in moves:
                     pass_on(part, stage)
 
-        far_rows = far_of(item)
-        length = len_ref[item]
         key_at = lax.broadcasted_iota(jnp.int32, (keys_n, 2 * SPAN), 0)
         span_at = key_at - SPAN
-
-        def seen(sub):
+        spots = [(two * 2 + k, sub) for k in range(2) for sub in range(spans_here)]
+
+        def seen(item, sub):
             mine = sq_i * spans_here + sub
+            length = len_ref[item]
             near_ok = (key_at < SPAN) & (mine * SPAN + key_at < length)
             return near_ok | ((key_at >= SPAN) & (span_at * SPAN < length) & (span_at != mine))
 
         scores = []
-        for sub, pair in units:
+        for item, sub in spots:
             rows = rows_of(item, sub)
-            kk = both(rows, far_rows, cols_of(1, pair))
-            scores.append(mm(kk, by_head(qkv[rows, cols_of(0, pair)], query_a, query_b), NT))
-        for (sub, pair), score in zip(units, scores):
-            score = jnp.where(seen(sub), score, neg_fill)
-            raised = jnp.exp(score - jnp.max(score, axis=0, keepdims=True))
-            share = raised * (1.0 / jnp.sum(raised, axis=0, keepdims=True))
-            prob[item * spans_here + sub, pair] = share.astype(BF)
-        for sub in range(spans_here):
+            for pair in range(pairs):
+                kk = both(rows, far_of(item), cols_of(1, pair))
+                scores.append(mm(kk, by_head(qkv[rows, cols_of(0, pair)], query_a, query_b), NT))
+        for n, (item, sub) in enumerate(spots):
+            for pair in range(pairs):
+                score = jnp.where(seen(item, sub), scores[n * pairs + pair], neg_fill)
+                raised = jnp.exp(score - jnp.max(score, axis=0, keepdims=True))
+                share = raised * (1.0 / jnp.sum(raised, axis=0, keepdims=True))
+                prob[item * spans_here + sub, pair] = share.astype(BF)
+        for item, sub in spots:
             rows = rows_of(item, sub)
             mixed = []
             for pair in range(pairs):
-                vv = both(rows, far_rows, cols_of(2, pair))
+                vv = both(rows, far_of(item), cols_of(2, pair))
                 stacked = mm(vv, prob[item * spans_here + sub, pair], TN)
                 mixed += [stacked[0:HEAD_DIM, 0:SPAN], stacked[HEAD_DIM:, SPAN:]]
             mix[rows, :] = jnp.concatenate(mixed, axis=0).T.astype(BF)
 
-    each(items, attend)
+    each(items // 2, attend)
     for group in (*hops_kv, *hops_qo, direct_u, direct_d, pool_hops):
         sent(group)
 

time: 147 us -> 146 us (level)
  no operation moved by 1% of the time
where the time goes in v6:
time: 146 us
  Pallas kernels  145 us (99%)
    pallas_call x1, Pallas kernels, fused_device(): pl.pallas_call(layer_kernel, out_shape=[jax.ShapeDtypeStruct((rows_all, w...  138 us
    pallas_call x1, Pallas kernels, fused_device(): pl.pallas_call(update_kernel, out_shape=[jax.ShapeDtypeStruct((rows_all,...  7.14 us

profile of v6, /device:TPU:0, one launch (start us, length us, event | category | flops | bytes accessed | tf_op | source)
XLA Modules:
  0.0 146.3 jit_solution(10790577936356974917)
XLA Ops:
  0.7 138.3 %shard_map.313 = (bf16[2048,512]{1,0:T(8,128)(2,1)}, f32[2048,512]{1,0:T(8,128)}, f32[16,1536]{1,0:T(8,128)}, f32[16,512]{1,0:T(8,128)}, f32[16,2048]{1,0:T(8,12...) custom-call(s32[8]{0:T(128)} %len_ref.1, bf16[2048,512]{1,0:T(8,128)(2,1)} %bitcast.5, ...), custom_call_target="tpu_custom_call" | custom-call | tf_op jit(solution)/shard_map/pallas_call | solution.py:1264
  139.0 7.1 %shard_map.314 = (bf16[2048,512]{1,0:T(8,128)(2,1)}, f32[2048,512]{1,0:T(8,128)}, f32[1,1]{1,0:T(1,128)}, f32[16,1536]{1,0:T(8,128)}, f32[16,1536]{1,0:T(8,128)}...) custom-call(bf16[2048,512]{1,0:T(8,128)(2,1)} %get-tuple-element.44., ...), custom_call_target="tpu_custom_call" | custom-call | tf_op jit(solution)/shard_map/pallas_call | solution.py:1344
